TPU v7x, 32 devices: a whole 2x2x4 slice. The times are simulated.
32 devices in a mesh: wide: 16 (over z, y, x), narrow: 2 (over core).
Axes of the slice: x: 2, y: 2, z: 4, core: 2. Of those that a mesh axis runs over, the one named last changes fastest.
Arguments:
- live_counts: int32 [16, 3], P('wide'), may hold values from 2 to 4, as said below
- small_in: bfloat16 [64, 5, 5, 2048], P('wide', None, None, 'narrow'), may hold values from -8 to 8
- mid_in: bfloat16 [64, 6, 6, 2048], P('wide', None, None, 'narrow'), may hold values from -8 to 8
- big_in: bfloat16 [64, 7, 7, 2048], P('wide', None, None, 'narrow'), may hold values from -8 to 8
- conv_first: bfloat16 [2048, 512], P(None, 'narrow'), may hold values from -0.125 to 0.125
- conv_middle: bfloat16 [4608, 512], P(None, 'narrow'), may hold values from -0.09375 to 0.09375
- conv_last: bfloat16 [512, 2048], P(None, 'narrow'), may hold values from -0.25 to 0.25
- gain_first: float32 [512], P('narrow'), may hold values from 0.5 to 1.5
- shift_first: float32 [512], P('narrow'), may hold values from -3 to 3
- gain_middle: float32 [512], P('narrow'), may hold values from 0.5 to 1.5
- shift_middle: float32 [512], P('narrow'), may hold values from -3 to 3
- gain_last: float32 [2048], P('narrow'), may hold values from 0.5 to 1.5
- shift_last: float32 [2048], P('narrow'), may hold values from -3 to 3
- small_cot: bfloat16 [64, 5, 5, 2048], P('wide', None, None, 'narrow'), may hold values from -6 to 6
- mid_cot: bfloat16 [64, 6, 6, 2048], P('wide', None, None, 'narrow'), may hold values from -6 to 6
- big_cot: bfloat16 [64, 7, 7, 2048], P('wide', None, None, 'narrow'), may hold values from -6 to 6
Outputs:
- small_out: bfloat16 [64, 5, 5, 2048], P('wide', None, None, 'narrow')
- mid_out: bfloat16 [64, 6, 6, 2048], P('wide', None, None, 'narrow')
- big_out: bfloat16 [64, 7, 7, 2048], P('wide', None, None, 'narrow')
- small_grad: bfloat16 [64, 5, 5, 2048], P('wide', None, None, 'narrow')
- mid_grad: bfloat16 [64, 6, 6, 2048], P('wide', None, None, 'narrow')
- big_grad: bfloat16 [64, 7, 7, 2048], P('wide', None, None, 'narrow')
- first_grad: float32 [2048, 512], P('wide', 'narrow')
- middle_grad: float32 [4608, 512], P('wide', 'narrow')
- last_grad: float32 [512, 2048], P('wide', 'narrow')
- gain_first_grad: float32 [512], P('narrow')
- shift_first_grad: float32 [512], P('narrow')
- gain_middle_grad: float32 [512], P('narrow')
- shift_middle_grad: float32 [512], P('narrow')
- gain_last_grad: float32 [2048], P('narrow')
- shift_last_grad: float32 [2048], P('narrow')
Inputs may be any that keep to these rules, and one draw needn't show every extreme that they name: `live_counts`: every device has between (4 + 1) // 2 and 4 live images of each resolution, the live ones first; in every draw some device is full in all three groups and another holds (4 + 1) // 2 in all three.
All inputs are finite; a program needn't handle non-finite values.
Results may differ from a plain program's by a relative error of at most 0.02.
Values may be sent and summed in bfloat16 or wider, within the bound.
A program may use at most 128 MiB of HBM per device.

v0:
```python
import jax
import jax.numpy as jnp
from jax import lax
from jax.sharding import PartitionSpec as P

epsilon = 1e-05


def smooth(values):
    return jax.nn.gelu(values, approximate=False)


def smooth_slope(values, upstream):
    unused, pullback = jax.vjp(smooth, values)
    return pullback(upstream)[0]


def channel_sum(tensors, masks):
    return sum(
        (jnp.sum(tensor * part_mask, axis=(0, 1, 2)) for tensor, part_mask in zip(tensors, masks))
    )


def moments(values, masks, count_local):
    total_sum, count = lax.psum((channel_sum(values, masks), count_local), "wide")
    centre = total_sum / count
    deviations = [jnp.square(tensor - centre) for tensor in values]
    spread = lax.psum(channel_sum(deviations, masks), "wide") / count
    return (centre, lax.rsqrt(spread + epsilon), count)


def gather_hidden(tensors):
    return (
        lax.all_gather(tensors[0], "narrow", axis=3, tiled=True),
        lax.all_gather(tensors[1], "narrow", axis=3, tiled=True),
        lax.all_gather(tensors[2], "narrow", axis=3, tiled=True),
    )


def scatter_hidden(tensors):
    return (
        lax.psum_scatter(
            tensors[0].astype(jnp.bfloat16), "narrow", scatter_dimension=3, tiled=True
        ).astype(jnp.float32),
        lax.psum_scatter(
            tensors[1].astype(jnp.bfloat16), "narrow", scatter_dimension=3, tiled=True
        ).astype(jnp.float32),
        lax.psum_scatter(
            tensors[2].astype(jnp.bfloat16), "narrow", scatter_dimension=3, tiled=True
        ).astype(jnp.float32),
    )


def norm_back(upstream, normed, scaled, gain, masks, count):
    crossed = [grad * value for grad, value in zip(upstream, normed)]
    total_grad, total_cross = lax.psum(
        (channel_sum(upstream, masks), channel_sum(crossed, masks)), "wide"
    )
    factor = gain * scaled
    slopes = [
        (part_mask * factor * (grad - total_grad / count - value * total_cross / count)).astype(
            jnp.bfloat16
        )
        for grad, value, part_mask in zip(upstream, normed, masks)
    ]
    return (slopes, total_cross, total_grad)


def project(tensor, weight):
    flat = jnp.dot(tensor.reshape(-1, tensor.shape[-1]), weight, preferred_element_type=jnp.float32)
    return flat.reshape(tensor.shape[:3] + (weight.shape[1],))


def project_back(tensor, weight):
    flat = lax.dot_general(
        tensor.reshape(-1, tensor.shape[-1]),
        weight,
        (((1,), (1,)), ((), ())),
        preferred_element_type=jnp.float32,
    )
    return flat.reshape(tensor.shape[:3] + (weight.shape[0],))


def flat_dot(left, right):
    return lax.dot_general(
        left.reshape(-1, left.shape[-1]),
        right.reshape(-1, right.shape[-1]),
        (((0,), (0,)), ((), ())),
        preferred_element_type=jnp.float32,
    )


def patches(tensor):
    height, width = (tensor.shape[1], tensor.shape[2])
    padded = jnp.pad(tensor, ((0, 0), (1, 1), (1, 1), (0, 0)))
    return jnp.concatenate(
        [
            padded[:, offset_y : offset_y + height, offset_x : offset_x + width, :]
            for offset_y in range(3)
            for offset_x in range(3)
        ],
        axis=3,
    )


def fold_patches(columns, channels):
    images, height, width = (columns.shape[0], columns.shape[1], columns.shape[2])
    padded = jnp.zeros((images, height + 2, width + 2, channels), jnp.float32)
    for offset_y in range(3):
        for offset_x in range(3):
            kernel_pos = offset_y * 3 + offset_x
            padded = padded.at[:, offset_y : offset_y + height, offset_x : offset_x + width, :].add(
                columns[..., kernel_pos * channels : (kernel_pos + 1) * channels]
            )
    return padded[:, 1:-1, 1:-1, :]


def local(
    live_counts,
    small_in,
    mid_in,
    big_in,
    conv_first,
    conv_middle,
    conv_last,
    gain_first,
    shift_first,
    gain_middle,
    shift_middle,
    gain_last,
    shift_last,
    small_cot,
    mid_cot,
    big_cot,
):
    inputs = (small_in, mid_in, big_in)
    cots = (small_cot, mid_cot, big_cot)
    masks = [
        (jnp.arange(tensor.shape[0]) < live_counts[0, column]).astype(jnp.float32)[
            :, None, None, None
        ]
        for column, tensor in enumerate(inputs)
    ]
    count_local = sum(
        (
            jnp.sum(part_mask) * (tensor.shape[1] * tensor.shape[2])
            for tensor, part_mask in zip(inputs, masks)
        )
    )
    full_inputs = (
        lax.all_gather(small_in, "narrow", axis=3, tiled=True),
        lax.all_gather(mid_in, "narrow", axis=3, tiled=True),
        lax.all_gather(big_in, "narrow", axis=3, tiled=True),
    )
    first = [project(tensor, conv_first) for tensor in full_inputs]
    centre_one, scaled_one, count = moments(first, masks, count_local)
    normed_one = [(tensor - centre_one) * scaled_one for tensor in first]
    act_one = [tensor * gain_first + shift_first for tensor in normed_one]
    full_one = gather_hidden([smooth(tensor).astype(jnp.bfloat16) for tensor in act_one])
    columns = [patches(tensor) for tensor in full_one]
    second = [project(tensor, conv_middle) for tensor in columns]
    centre_two, scaled_two, count_two = moments(second, masks, count_local)
    normed_two = [(tensor - centre_two) * scaled_two for tensor in second]
    act_two = [tensor * gain_middle + shift_middle for tensor in normed_two]
    full_two = gather_hidden([smooth(tensor).astype(jnp.bfloat16) for tensor in act_two])
    third = [project(tensor, conv_last) for tensor in full_two]
    centre_three, scaled_three, count_three = moments(third, masks, count_local)
    normed_three = [(tensor - centre_three) * scaled_three for tensor in third]
    before = [
        tensor * gain_last + shift_last + image.astype(jnp.float32)
        for tensor, image in zip(normed_three, inputs)
    ]
    outputs = [
        (part_mask * smooth(tensor)).astype(jnp.bfloat16)
        for tensor, part_mask in zip(before, masks)
    ]
    upstream = [
        smooth_slope(tensor, cot.astype(jnp.float32) * part_mask)
        for tensor, cot, part_mask in zip(before, cots, masks)
    ]
    slope_three, gain_last_grad, shift_last_grad = norm_back(
        upstream, normed_three, scaled_three, gain_last, masks, count
    )
    last_grad = sum((flat_dot(full, slope) for full, slope in zip(full_two, slope_three)))
    back_two = scatter_hidden([project_back(slope, conv_last) for slope in slope_three])
    up_two = [smooth_slope(act, back) for act, back in zip(act_two, back_two)]
    slope_two, gain_middle_grad, shift_middle_grad = norm_back(
        up_two, normed_two, scaled_two, gain_middle, masks, count
    )
    middle_grad = sum((flat_dot(cols, slope) for cols, slope in zip(columns, slope_two)))
    channels = conv_middle.shape[0] // 9
    back_one = scatter_hidden(
        [fold_patches(project_back(slope, conv_middle), channels) for slope in slope_two]
    )
    up_one = [smooth_slope(act, back) for act, back in zip(act_one, back_one)]
    slope_one, gain_first_grad, shift_first_grad = norm_back(
        up_one, normed_one, scaled_one, gain_first, masks, count
    )
    first_grad = sum((flat_dot(full, slope) for full, slope in zip(full_inputs, slope_one)))
    input_back = (
        lax.psum_scatter(
            project_back(slope_one[0], conv_first).astype(jnp.bfloat16),
            "narrow",
            scatter_dimension=3,
            tiled=True,
        ).astype(jnp.float32),
        lax.psum_scatter(
            project_back(slope_one[1], conv_first).astype(jnp.bfloat16),
            "narrow",
            scatter_dimension=3,
            tiled=True,
        ).astype(jnp.float32),
        lax.psum_scatter(
            project_back(slope_one[2], conv_first).astype(jnp.bfloat16),
            "narrow",
            scatter_dimension=3,
            tiled=True,
        ).astype(jnp.float32),
    )
    input_grads = [(grad + back).astype(jnp.bfloat16) for grad, back in zip(upstream, input_back)]
    first_grad, middle_grad, last_grad = (
        lax.psum_scatter(first_grad, "wide", scatter_dimension=0, tiled=True),
        lax.psum_scatter(middle_grad, "wide", scatter_dimension=0, tiled=True),
        lax.psum_scatter(last_grad, "wide", scatter_dimension=0, tiled=True),
    )
    return (
        outputs[0],
        outputs[1],
        outputs[2],
        input_grads[0],
        input_grads[1],
        input_grads[2],
        first_grad,
        middle_grad,
        last_grad,
        gain_first_grad,
        shift_first_grad,
        gain_middle_grad,
        shift_middle_grad,
        gain_last_grad,
        shift_last_grad,
    )


def solution(mesh):
    placed = (
        P("wide", None),
        P("wide", None, None, "narrow"),
        P("wide", None, None, "narrow"),
        P("wide", None, None, "narrow"),
        P(None, "narrow"),
        P(None, "narrow"),
        P(None, "narrow"),
        P("narrow"),
        P("narrow"),
        P("narrow"),
        P("narrow"),
        P("narrow"),
        P("narrow"),
        P("wide", None, None, "narrow"),
        P("wide", None, None, "narrow"),
        P("wide", None, None, "narrow"),
    )
    return jax.shard_map(
        local,
        mesh=mesh,
        in_specs=placed,
        out_specs=(
            P("wide", None, None, "narrow"),
            P("wide", None, None, "narrow"),
            P("wide", None, None, "narrow"),
            P("wide", None, None, "narrow"),
            P("wide", None, None, "narrow"),
            P("wide", None, None, "narrow"),
            P("wide", "narrow"),
            P("wide", "narrow"),
            P("wide", "narrow"),
            P("narrow"),
            P("narrow"),
            P("narrow"),
            P("narrow"),
            P("narrow"),
            P("narrow"),
        ),
        check_vma=False,
    )
```

profile of v0, /device:TPU:0, one launch (start us, length us, event | category | flops | bytes accessed | tf_op | source)
XLA Modules:
  0.0 911.0 jit_solution(7845702570141402408)
XLA Ops:
  30.5 44.0 %all-reduce.9 = (f32[256]{0:T(256)S(1)}, f32[]{:T(128)}) all-reduce(f32[256]{0:T(256)S(1)} %add_add_fusion.11, f32[]{:T(128)S(6)} %add.452), channel_id=1, replica_groups=mesh['wide'=16,'narrow'=2] {'wide'}, use_global_device_ids=true, to_apply=%region_3.0 | all-reduce | flops 257 | bytes 2056 | tf_op jit(solution)/shard_map/psum | solution.py:25
  78.3 36.6 %psum.99 = f32[256]{0:T(256)S(1)} all-reduce(f32[256]{0:T(256)S(1)} %add_add_fusion.10), channel_id=1, replica_groups=mesh['wide'=16,'narrow'=2] {'wide'}, use_global_device_ids=true, to_apply=%region_11.0 | all-reduce | flops 256 | bytes 2048 | tf_op jit(solution)/shard_map/psum | solution.py:28
  134.8 38.8 %psum.100 = f32[256]{0:T(256)S(1)} all-reduce(f32[256]{0:T(256)S(1)} %add_add_fusion.9), channel_id=1, replica_groups=mesh['wide'=16,'narrow'=2] {'wide'}, use_global_device_ids=true, to_apply=%region_15.16 | all-reduce | flops 256 | bytes 2048 | tf_op jit(solution)/shard_map/psum | solution.py:25
  177.3 36.6 %psum.101 = f32[256]{0:T(256)S(1)} all-reduce(f32[256]{0:T(256)S(1)} %add_add_fusion.8), channel_id=1, replica_groups=mesh['wide'=16,'narrow'=2] {'wide'}, use_global_device_ids=true, to_apply=%region_19.20 | all-reduce | flops 256 | bytes 2048 | tf_op jit(solution)/shard_map/psum | solution.py:28
  230.8 38.6 %psum.102 = f32[1024]{0:T(1024)S(1)} all-reduce(f32[1024]{0:T(1024)S(1)} %add_add_fusion.3), channel_id=1, replica_groups=mesh['wide'=16,'narrow'=2] {'wide'}, use_global_device_ids=true, to_apply=%region_23.24 | all-reduce | flops 1024 | bytes 8192 | tf_op jit(solution)/shard_map/psum | solution.py:25
  273.0 36.6 %psum.103 = f32[1024]{0:T(1024)S(1)} all-reduce(f32[1024]{0:T(1024)S(1)} %add_add_fusion.2), channel_id=1, replica_groups=mesh['wide'=16,'narrow'=2] {'wide'}, use_global_device_ids=true, to_apply=%region_27.28 | all-reduce | flops 1024 | bytes 8192 | tf_op jit(solution)/shard_map/psum | solution.py:28
  310.5 4.1 multiply_reduce_fusion.9
  314.6 3.2 multiply_reduce_fusion.5
  317.9 3.7 multiply_reduce_fusion.1
  321.6 39.1 %all-reduce.8 = (f32[1024]{0:T(1024)S(1)}, f32[1024]{0:T(1024)S(1)}) all-reduce(f32[1024]{0:T(1024)S(1)} %add_add_fusion, f32[1024]{0:T(1024)S(1)} %add_add_fusion.1), channel_id=1, replica_groups=mesh['wide'=16,'narrow'=2] {'wide'}, use_global_device_ids=true, to_apply=%region_35.36 | all-reduce | flops 2048 | bytes 16384 | tf_op jit(solution)/shard_map/psum | solution.py:56
  361.4 3.3 multiply_convert_fusion.4
  366.7 3.6 multiply_convert_fusion.2
  372.3 3.8 multiply_convert_fusion
  383.4 8.8 reduce-scatter.17.cloned.1.call-done
  394.2 42.1 %all-reduce.7 = (f32[256]{0:T(256)S(1)}, f32[256]{0:T(256)S(1)}) all-reduce(f32[256]{0:T(256)S(1)} %add_add_fusion.6, f32[256]{0:T(256)S(1)} %add_add_fusion.7), channel_id=1, replica_groups=mesh['wide'=16,'narrow'=2] {'wide'}, use_global_device_ids=true, to_apply=%region_46.47 | all-reduce | flops 512 | bytes 4096 | tf_op jit(solution)/shard_map/psum | solution.py:56
  451.9 2.9 add_select_fusion.2
  472.4 3.0 add_select_fusion.1
  494.0 3.0 add_select_fusion
  518.1 6.5 reduce-scatter.23.cloned.1.call-done
  525.8 41.9 %all-reduce.6 = (f32[256]{0:T(256)S(1)}, f32[256]{0:T(256)S(1)}) all-reduce(f32[256]{0:T(256)S(1)} %add_add_fusion.4, f32[256]{0:T(256)S(1)} %add_add_fusion.5), channel_id=1, replica_groups=mesh['wide'=16,'narrow'=2] {'wide'}, use_global_device_ids=true, to_apply=%region_58.59 | all-reduce | flops 512 | bytes 4096 | tf_op jit(solution)/shard_map/psum | solution.py:56
  588.6 3.4 fusion
  602.6 80.1 %reduce-scatter.31.cloned.1.call-done = f32[128,256]{0,1:T(8,128)} async-done(((f32[2048,256]{0,1:T(8,128)}), f32[128,256]{0,1:T(8,128)}) %reduce-scatter.31.cloned.1.call-update) | async-done | bytes 131088 | tf_op jit(solution)/shard_map/reduce_scatter | solution.py:222
  684.3 78.6 %reduce-scatter.35.cloned.1.call-done = f32[32,1024]{1,0:T(8,128)} async-done(((f32[512,1024]{1,0:T(8,128)}), f32[32,1024]{1,0:T(8,128)}) %reduce-scatter.35.cloned.1.call-update) | async-done | bytes 131088 | tf_op jit(solution)/shard_map/reduce_scatter | solution.py:224
  763.0 140.7 %reduce-scatter.33.cloned.1.call-done = f32[288,256]{1,0:T(8,128)} async-done(((f32[4608,256]{1,0:T(8,128)}), f32[288,256]{1,0:T(8,128)}) %reduce-scatter.33.cloned.1.call-update) | async-done | bytes 294928 | tf_op jit(solution)/shard_map/reduce_scatter | solution.py:223
  (366 shorter events, 190.0 us)
Async XLA Ops:
  7.2 121.3 %copy-start = (bf16[4608,256]{1,0:T(8,128)(2,1)S(1)}, bf16[4608,256]{1,0:T(8,128)(2,1)}, u32[]{:S(2)}) copy-start(bf16[4608,256]{1,0:T(8,128)(2,1)} %param.75) | copy-start | bytes 7077892
  7.2 373.7 %reduce-scatter.13.cloned.1.call-start = ((), (), s32[]{:S(2)}) async-start(), calls=%async_computation.12 | async-start | bytes 245760 | tf_op jit(solution)/shard_map/reduce_scatter | solution.py:42
  28.0 86.9 %copy-start.55 = (f32[256]{0:T(256)S(1)}, f32[256]{0:T(256)}, u32[]{:S(2)}) copy-start(f32[256]{0:T(256)} %param.77) | copy-start | bytes 3076
  28.0 87.6 %copy-start.58 = (f32[256]{0:T(256)S(1)}, f32[256]{0:T(256)}, u32[]{:S(2)}) copy-start(f32[256]{0:T(256)} %param.78) | copy-start | bytes 3076
  132.7 81.2 %copy-start.54 = (f32[256]{0:T(256)S(1)}, f32[256]{0:T(256)}, u32[]{:S(2)}) copy-start(f32[256]{0:T(256)} %param.79) | copy-start | bytes 3076
  132.7 81.9 %copy-start.57 = (f32[256]{0:T(256)S(1)}, f32[256]{0:T(256)}, u32[]{:S(2)}) copy-start(f32[256]{0:T(256)} %param.80) | copy-start | bytes 3076
  134.7 92.0 %copy-start.2 = (bf16[512,1024]{1,0:T(8,128)(2,1)S(1)}, bf16[512,1024]{1,0:T(8,128)(2,1)}, u32[]{:S(2)}) copy-start(bf16[512,1024]{1,0:T(8,128)(2,1)} %param.76) | copy-start | bytes 3145732
  229.3 80.2 %copy-start.52 = (f32[1024]{0:T(1024)S(1)}, f32[1024]{0:T(1024)}, u32[]{:S(2)}) copy-start(f32[1024]{0:T(1024)} %param.81) | copy-start | bytes 12292
  229.3 81.1 %copy-start.53 = (f32[1024]{0:T(1024)S(1)}, f32[1024]{0:T(1024)}, u32[]{:S(2)}) copy-start(f32[1024]{0:T(1024)} %param.82) | copy-start | bytes 12292
  366.6 15.5 %reduce-scatter.15.cloned.1.call-start = ((), (), s32[]{:S(2)}) async-start(), calls=%async_computation.13 | async-start | bytes 294912 | tf_op jit(solution)/shard_map/reduce_scatter | solution.py:45
  372.2 20.0 %reduce-scatter.17.cloned.1.call-start = ((), (), s32[]{:S(2)}) async-start(), calls=%async_computation.14 | async-start | bytes 344064 | tf_op jit(solution)/shard_map/reduce_scatter | solution.py:48
  378.2 58.9 %copy-start.25 = (f32[4,5,5,256]{3,2,1,0:T(8,128)S(1)}, f32[4,5,5,256]{3,2,1,0:T(8,128)}, u32[]{:S(2)}) copy-start(f32[4,5,5,256]{3,2,1,0:T(8,128)} %get-tuple-element.444) | copy-start | bytes 307204
  378.2 137.5 %reduce-scatter.19.cloned.1.call-start = ((), (), s32[]{:S(2)}) async-start(), calls=%async_computation.15 | async-start | bytes 245760 | tf_op jit(solution)/shard_map/reduce_scatter | solution.py:42
  470.0 46.9 %reduce-scatter.21.cloned.1.call-start = ((), (), s32[]{:S(2)}) async-start(), calls=%async_computation.16 | async-start | bytes 294912 | tf_op jit(solution)/shard_map/reduce_scatter | solution.py:45
  509.5 15.1 %reduce-scatter.23.cloned.1.call-start = ((), (), s32[]{:S(2)}) async-start(), calls=%async_computation.17 | async-start | bytes 344064 | tf_op jit(solution)/shard_map/reduce_scatter | solution.py:48
  513.3 55.2 %copy-start.66 = (f32[4,256]{1,0:T(4,128)S(1)}, f32[4,256]{1,0:T(4,128)}, u32[]{:S(2)}) copy-start(f32[4,256]{1,0:T(4,128)} %get-tuple-element.424) | copy-start | bytes 12292
  513.3 55.9 %copy-start.4 = (bf16[2048,256]{1,0:T(8,128)(2,1)S(1)}, bf16[2048,256]{1,0:T(8,128)(2,1)}, u32[]{:S(2)}) copy-start(bf16[2048,256]{1,0:T(8,128)(2,1)} %param.74) | copy-start | bytes 3145732
  515.4 80.4 %reduce-scatter.25.cloned.1.call-start = ((), (), s32[]{:S(2)}) async-start(), calls=%async_computation.18 | async-start | bytes 983040 | tf_op jit(solution)/shard_map/reduce_scatter | solution.py:201
  570.6 27.3 %reduce-scatter.27.cloned.1.call-start = ((), (), s32[]{:S(2)}) async-start(), calls=%async_computation.19 | async-start | bytes 1179648 | tf_op jit(solution)/shard_map/reduce_scatter | solution.py:207
  572.8 27.5 %reduce-scatter.29.cloned.1.call-start = ((), (), s32[]{:S(2)}) async-start(), calls=%async_computation.20 | async-start | bytes 1376256 | tf_op jit(solution)/shard_map/reduce_scatter | solution.py:213
  575.2 107.5 %reduce-scatter.31.cloned.1.call-start = ((), (), s32[]{:S(2)}) async-start(), calls=%async_computation.21 | async-start | bytes 2228224 | tf_op jit(solution)/shard_map/reduce_scatter | solution.py:222
  579.4 183.6 %reduce-scatter.35.cloned.1.call-start = ((), (), s32[]{:S(2)}) async-start(), calls=%async_computation.23 | async-start | bytes 2228224 | tf_op jit(solution)/shard_map/reduce_scatter | solution.py:224
  584.1 319.6 %reduce-scatter.33.cloned.1.call-start = ((), (), s32[]{:S(2)}) async-start(), calls=%async_computation.22 | async-start | bytes 5013504 | tf_op jit(solution)/shard_map/reduce_scatter | solution.py:223
  597.9 305.8 %copy-start.1 = (bf16[4608,256]{1,0:T(8,128)(2,1)S(1)}, bf16[4608,256]{1,0:T(8,128)(2,1)}, u32[]{:S(2)}) copy-start(bf16[4608,256]{1,0:T(8,128)(2,1)} %param.75) | copy-start | bytes 7077892
  (61 other events, 273.5 us)
Sparse Core Ops, SparseCore 0:
  366.7 3.4 reduce-scatter.12
  372.4 8.7 reduce-scatter.14
  383.5 8.7 reduce-scatter.16
  470.1 3.3 reduce-scatter.18
  509.6 3.4 reduce-scatter.20
  515.7 8.7 reduce-scatter.22
  570.7 3.9 reduce-scatter.24
  577.1 9.3 reduce-scatter.26
  588.7 9.5 reduce-scatter.28
  600.5 82.0 reduce-scatter.30
  685.6 77.2 reduce-scatter.34
  769.4 134.2 reduce-scatter.32
where the time goes:
time: 922 us; the launch traced here: 911 us
  blocking collectives  374 us (41%)
  waiting for transfers between devices  315 us (34%)
  other arithmetic  109 us (12%)
  local copies, waits for them, and re-layouts  57.4 us (6%)
  matrix products  37 us (4%)
  between operations  18 us (2%)
    reduce_scatter x1, waiting for transfers between devices, local(): lax.psum_scatter(middle_grad, 'wide', scatter_dimension=0, tiled=True)  141 us
    psum x3, blocking collectives, norm_back(): lax.psum((channel_sum(upstream, masks), channel_sum(crossed, masks)), 'wi...  123 us
    psum x3, blocking collectives, moments(): lax.psum((channel_sum(values, masks), count_local), 'wide')  121 us
    psum x3, blocking collectives, moments(): spread = lax.psum(channel_sum(deviations, masks), 'wide') / count  110 us
    reduce_scatter x1, waiting for transfers between devices, local(): lax.psum_scatter(first_grad, 'wide', scatter_dimension=0, tiled=True)  80.1 us
    reduce_scatter x1, waiting for transfers between devices, local(): lax.psum_scatter(last_grad, 'wide', scatter_dimension=0, tiled=True)  78.6 us
    scatter-add x27, local copies, waits for them, and re-layouts, fold_patches(): padded.at[:, offset_y:offset_y + height, offset_x:offset_x + width, :]  33.1 us
    reduce_sum x18, other arithmetic, channel_sum(): jnp.sum(tensor * part_mask, axis=(0, 1, 2))  28.1 us
  transfers between devices with their start and end apart: 12, of which 5 were waited for; matrix products, arithmetic and copies ran while one was open for 10% of the time, Pallas kernels for 0%

commit v1 on v0

v1 whole, which is shorter than its diff:
```python
import functools

import jax
import jax.numpy as jnp
from jax import lax
from jax.experimental import pallas as pl
from jax.experimental.pallas import tpu as pltpu
from jax.sharding import PartitionSpec as P

MESH = pl.DeviceIdType.MESH
EPSILON = 1e-05
F32 = jnp.float32
BF16 = jnp.bfloat16
LANES = 128
CHUNK = 16
GUARD = 64


def ceil_to(value, step):
    return (value + step - 1) // step * step


class Geometry:
    def __init__(self, wide, shapes, channels, hidden, half):
        self.wide = wide
        self.slots = shapes[0][0]
        self.sides = [(shape[1], shape[2]) for shape in shapes]
        self.pixels = [height * width for height, width in self.sides]
        self.real = [count * self.slots for count in self.pixels]
        self.padded = [ceil_to(count, CHUNK) for count in self.real]
        self.starts = [sum(self.padded[:index]) for index in range(len(shapes))]
        self.rows = sum(self.padded)
        self.chunks = self.rows // CHUNK
        self.channels = channels
        self.hidden = hidden
        self.half = half
        self.wide_half = channels // 2
        self.shares = (hidden // wide, 9 * hidden // wide, channels // wide)
        bits = wide.bit_length() - 1
        self.bits = bits
        self.scattered = (
            wide >= 8 and wide == 1 << bits and all(share % CHUNK == 0 for share in self.shares)
        )


def span(start, size):
    return pl.ds(pl.multiple_of(start, size), size)


def dot(left, right):
    return lax.dot_general(left, right, (((1,), (0,)), ((), ())), preferred_element_type=F32)


def dot_turned(left, right):
    return lax.dot_general(left, right, (((1,), (1,)), ((), ())), preferred_element_type=F32)


def gelu_parts(value):
    share = 0.5 + 0.5 * lax.erf(value * 0.7071067811865476)
    slope = share + value * (jnp.exp(value * value * -0.5) * 0.3989422804014327)
    return share, slope


def block_kernel(geo, *refs):
    refs = list(refs)

    def take(count):
        taken = refs[:count]
        del refs[:count]
        return taken

    (live_counts,) = take(1)
    inputs = take(3)
    first_hbm, middle_hbm, last_hbm = take(3)
    affine_hbm = take(6)
    cots = take(3)
    outs = take(3)
    in_grads = take(3)
    weight_outs = take(3)
    affine_outs = take(6)
    raw_x, raw_cot, raw_out, raw_grad = take(3), take(3), take(3), take(3)
    conv_first, conv_middle, conv_last = take(3)
    affine = take(6)
    live, shift_masks = take(2)
    x_all, x_turned, cot_rows = take(3)
    norm_one, norm_two, norm_three = take(3)
    slope_act_one, slope_act_two = take(2)
    hidden_one, hidden_two, turned_one, turned_two = take(4)
    parts, shifted_src, shifted = take(3)
    up_three, out_rows, up_two, up_one = take(4)
    slope_three, slope_two, slope_one = take(3)
    send_two, recv_two, send_one, recv_one, send_in, recv_in = take(6)
    stat_bufs = take(6)
    totals = take(3)
    staged = [take(6) for _ in range(3)] if geo.scattered else None
    weight_stage = take(3)
    affine_stage = take(6)
    load_sem, out_sem, sib_send, sib_recv, stat_send, stat_recv = take(6)
    rs_send, rs_recv = take(2) if geo.scattered else (None, None)
    assert not refs

    wide, slots, half = geo.wide, geo.slots, geo.half
    me = lax.axis_index("wide")
    core = lax.axis_index("narrow")
    other = 1 - core

    loads = {}

    def load(name, source, target):
        loads[name] = pltpu.make_async_copy(source, target, load_sem.at[len(loads)])
        loads[name].start()

    for group in range(3):
        load(("x", group), inputs[group], raw_x[group])
    load("first", first_hbm, conv_first)
    for index in range(6):
        load(("affine", index), affine_hbm[index], affine[index])
    load("middle", middle_hbm, conv_middle)
    load("last", last_hbm, conv_last)
    for group in range(3):
        load(("cot", group), cots[group], raw_cot[group])

    barrier = pltpu.get_barrier_semaphore()

    def greet(index, carry):
        peer = lax.rem(me + 1 + index, wide)
        pl.semaphore_signal(barrier, inc=1, device_id=(peer, core), device_id_type=MESH)
        return carry

    lax.fori_loop(0, wide - 1, greet, 0)
    pl.semaphore_signal(barrier, inc=1, device_id=(me, other), device_id_type=MESH)

    local_count = 0
    for group in range(3):
        rows = geo.padded[group]
        limit = live_counts[0, group]
        local_count = local_count + limit * geo.pixels[group]
        index = lax.broadcasted_iota(jnp.int32, (rows, LANES), 0)
        image = index % slots
        mask = jnp.where((index < geo.real[group]) & (image < limit), 1.0, 0.0)
        live[geo.starts[group] : geo.starts[group] + rows, :] = mask
    count_here = jnp.full((1, LANES), local_count, jnp.int32).astype(F32)

    shift_masks[...] = jnp.ones_like(shift_masks)
    for group in range(3):
        height, width = geo.sides[group]
        start = geo.starts[group]
        line = width * slots
        for position in range(9):
            down, right = position // 3 - 1, position % 3 - 1
            if down == -1:
                shift_masks[position, start : start + line, :] = jnp.zeros((line, LANES), F32)
            if down == 1:
                low = start + (height - 1) * line
                shift_masks[position, low : low + line, :] = jnp.zeros((line, LANES), F32)
            if right:
                for row in range(height):
                    low = start + row * line + (0 if right == -1 else line - slots)
                    shift_masks[position, low : low + slots, :] = jnp.zeros((slots, LANES), F32)
    for buffer in (parts,):
        for position in range(9):
            buffer[position, 0:GUARD, :] = jnp.zeros((GUARD, half), F32)
            buffer[position, GUARD + geo.rows :, :] = jnp.zeros((GUARD, half), F32)
    shifted_src[0:GUARD, :] = jnp.zeros((GUARD, half), F32)
    shifted_src[GUARD + geo.rows :, :] = jnp.zeros((GUARD, half), F32)

    def spread(tile, width):
        return jnp.concatenate([tile] * (width // LANES), axis=1)

    def live_rows(rows, width):
        return spread(live[rows, :], width)

    def over_rows(body, init, unroll=1):
        return lax.fori_loop(
            0, geo.chunks, lambda step, carry: body(span(step * CHUNK, CHUNK), carry), init, unroll=unroll
        )

    def fold_rows(value):
        return sum(value[index * 8 : index * 8 + 8] for index in range(CHUNK // 8))

    def column_sum(value):
        return jnp.sum(value, axis=0, keepdims=True)

    to_other = {"device_id": (me, other), "device_id_type": MESH}

    def sibling(index, source, target):
        return pltpu.make_async_remote_copy(
            src_ref=source, dst_ref=target, send_sem=sib_send.at[index], recv_sem=sib_recv.at[index], **to_other
        )

    x_copies = []
    pl_wait_done = False
    for group in range(3):
        loads[("x", group)].wait()
        rows, real, start = geo.padded[group], geo.real[group], geo.starts[group]
        value = raw_x[group][...].astype(F32).reshape(real, geo.wide_half)
        if rows > real:
            value = jnp.concatenate([value, jnp.zeros((rows - real, geo.wide_half), F32)], axis=0)
        mask = spread(live[start : start + rows, :], geo.wide_half)
        place = x_all.at[core, pl.ds(start, rows)]
        place[...] = (value * mask).astype(BF16)
        if not pl_wait_done:
            pl.semaphore_wait(barrier, wide)
            pl_wait_done = True
        copy = sibling(group, place, place)
        copy.start()
        x_copies.append(copy)

    loads["first"].wait()
    norm_one[...] = dot(x_all[core], conv_first[span(core * geo.wide_half, geo.wide_half), :])
    for copy in x_copies:
        copy.wait_recv()
    norm_one[...] += dot(x_all[other], conv_first[span(other * geo.wide_half, geo.wide_half), :])

    def broadcast(round_index):
        buffer = stat_bufs[round_index]

        def push(index, carry):
            peer = lax.rem(me + 1 + index, wide)
            pltpu.make_async_remote_copy(
                src_ref=buffer.at[me],
                dst_ref=buffer.at[me],
                send_sem=stat_send.at[round_index],
                recv_sem=stat_recv.at[round_index],
                device_id=(peer, core),
                device_id_type=MESH,
            ).start()
            return carry

        lax.fori_loop(0, wide - 1, push, 0)

    def stat_wait(round_index, sem):
        view = stat_bufs[round_index].at[pl.ds(0, wide - 1)]
        pltpu.make_async_copy(view, view, sem.at[round_index]).wait()

    def send_moments(round_index, values, width):
        def add(rows, carry):
            return carry + fold_rows(values[rows, :] * live_rows(rows, width))

        total = column_sum(over_rows(add, jnp.zeros((8, width), F32)))
        centre = total / spread(count_here, width)

        def add_square(rows, carry):
            gap = (values[rows, :] - centre) * live_rows(rows, width)
            return carry + fold_rows(gap * gap)

        squares = column_sum(over_rows(add_square, jnp.zeros((8, width), F32)))
        buffer = stat_bufs[round_index]
        buffer[me, 0:1, :] = total
        buffer[me, 1:2, :] = squares
        if round_index == 0:
            buffer[me, 2:3, :] = spread(count_here, width)
        broadcast(round_index)

    def counts(width):
        return [spread(stat_bufs[0][index, 2:3, 0:LANES], width) for index in range(wide)]

    def get_moments(round_index, width):
        stat_wait(round_index, stat_recv)
        buffer = stat_bufs[round_index]
        each = counts(width)
        total_count = sum(each)
        centre = sum(buffer[index, 0:1, :] for index in range(wide)) / total_count
        squares = jnp.zeros((1, width), F32)
        for index in range(wide):
            gap = buffer[index, 0:1, :] / each[index] - centre
            squares = squares + (buffer[index, 1:2, :] + each[index] * gap * gap)
        return centre, lax.rsqrt(squares / total_count + EPSILON), 1.0 / total_count

    def send_sums(round_index, first, second):
        buffer = stat_bufs[round_index]
        buffer[me, 0:1, :] = column_sum(first)
        buffer[me, 1:2, :] = column_sum(second)
        broadcast(round_index)

    def get_sums(round_index):
        stat_wait(round_index, stat_recv)
        buffer = stat_bufs[round_index]
        total = sum(buffer[index] for index in range(wide))
        return total[0:1, :], total[1:2, :]

    def activate(values, slope_act, hidden, centre, scale, gain, shift):
        def step(rows, carry):
            mask = live_rows(rows, half)
            normed = (values[rows, :] - centre) * scale
            values[rows, :] = normed
            act = normed * gain + shift
            share, slope = gelu_parts(act)
            hidden[core, rows, :] = (act * share * mask).astype(BF16)
            slope_act[rows, :] = slope * mask
            return carry

        over_rows(step, 0)

    def gather_shifted(source, position, group):
        width = geo.sides[group][1]
        shift = slots * ((position // 3 - 1) * width + position % 3 - 1)
        low = GUARD + geo.starts[group] + shift
        return source[low : low + geo.padded[group], :]

    def fold_parts(pick):
        results = []
        for group in range(3):
            start, rows = geo.starts[group], geo.padded[group]
            total = None
            for position in range(9):
                value = gather_shifted(parts.at[pick(position)], position, group)
                if position != 4:
                    value = value * spread(shift_masks[position, start : start + rows, :], half)
                total = value if total is None else total + value
            results.append(total)
        return results

    send_moments(0, norm_one, half)
    for index in range(2):
        x_turned[index * geo.wide_half : (index + 1) * geo.wide_half, :] = x_all[index].T
    for index in range(6):
        loads[("affine", index)].wait()
    gain_one, shift_one, gain_two, shift_two, gain_three, shift_three = (ref[...] for ref in affine)
    centre_one, scale_one, inverse = get_moments(0, half)
    activate(norm_one, slope_act_one, hidden_one, centre_one, scale_one, gain_one, shift_one)
    copy_one = sibling(3, hidden_one.at[core], hidden_one.at[core])
    copy_one.start()
    loads["middle"].wait()
    copy_one.wait_recv()

    whole = slice(GUARD, GUARD + geo.rows)
    for position in range(9):
        low = position * geo.hidden
        parts[position, whole, :] = dot(hidden_one[0], conv_middle[low : low + half, :]) + dot(
            hidden_one[1], conv_middle[low + half : low + geo.hidden, :]
        )
    for group, value in enumerate(fold_parts(lambda position: position)):
        norm_two[geo.starts[group] : geo.starts[group] + geo.padded[group], :] = value
    send_moments(1, norm_two, half)
    for index in range(2):
        turned_one[index * half : (index + 1) * half, :] = hidden_one[index].T
    for group in range(3):
        loads[("cot", group)].wait()
        rows, real, start = geo.padded[group], geo.real[group], geo.starts[group]
        value = raw_cot[group][...].astype(F32).reshape(real, geo.wide_half)
        if rows > real:
            value = jnp.concatenate([value, jnp.zeros((rows - real, geo.wide_half), F32)], axis=0)
        cot_rows[start : start + rows, :] = value * spread(live[start : start + rows, :], geo.wide_half)
    centre_two, scale_two, _ = get_moments(1, half)
    activate(norm_two, slope_act_two, hidden_two, centre_two, scale_two, gain_two, shift_two)
    copy_two = sibling(4, hidden_two.at[core], hidden_two.at[core])
    copy_two.start()
    loads["last"].wait()
    copy_two.wait_recv()
    norm_three[...] = dot(hidden_two[0], conv_last[0:half, :]) + dot(hidden_two[1], conv_last[half:, :])
    send_moments(2, norm_three, geo.wide_half)
    for index in range(2):
        turned_two[index * half : (index + 1) * half, :] = hidden_two[index].T
    centre_three, scale_three, inverse_wide = get_moments(2, geo.wide_half)

    def finish(rows, carry):
        grad_sum, cross_sum = carry
        normed = (norm_three[rows, :] - centre_three) * scale_three
        norm_three[rows, :] = normed
        before = normed * gain_three + shift_three + x_all[core, rows, :].astype(F32)
        share, slope = gelu_parts(before)
        out_rows[rows, :] = before * share * live_rows(rows, geo.wide_half)
        up = cot_rows[rows, :] * slope
        up_three[rows, :] = up
        return grad_sum + fold_rows(up), cross_sum + fold_rows(up * normed)

    zero_wide = jnp.zeros((8, geo.wide_half), F32)
    send_sums(3, *over_rows(finish, (zero_wide, zero_wide)))

    stores = []

    def store(source, target):
        copy = pltpu.make_async_copy(source, target, out_sem.at[len(stores)])
        copy.start()
        stores.append(copy)

    for group in range(3):
        start, real = geo.starts[group], geo.real[group]
        value = out_rows[start : start + real, :].reshape(geo.pixels[group], slots, geo.wide_half)
        raw_out[group][...] = value.astype(BF16)
        store(raw_out[group], outs[group])

    def slopes(up, normed, target, scale, gain, sums, inverse_count, width, plain=None):
        grad_total, cross_total = sums
        factor = gain * scale
        grad_mean, cross_mean = grad_total * inverse_count, cross_total * inverse_count

        def step(rows, carry):
            value = live_rows(rows, width) * (
                factor * (up[rows, :] - grad_mean - normed[rows, :] * cross_mean)
            )
            target[rows, :] = value.astype(BF16)
            if plain is not None:
                plain[pl.ds(pl.multiple_of(GUARD + rows.start, CHUNK), CHUNK), :] = value
            return carry

        over_rows(step, 0)

    def give_affine(index, sums):
        affine_stage[2 * index][...] = sums[1]
        affine_stage[2 * index + 1][...] = sums[0]
        for place in (2 * index, 2 * index + 1):
            store(affine_stage[place], affine_outs[place])

    def weigh(stage):
        if stage == 0:
            return 1 + core
        if stage == 1:
            return 2 - core
        return 1 << stage

    def owner(slot):
        place = me
        for stage in range(geo.bits):
            chosen = (slot // (1 << (geo.bits - 1 - stage))) % 2
            weight = weigh(stage)
            mine = (me // weight) % 2
            place = place + chosen * (1 - 2 * mine) * weight
        return place

    def owned(which, slot):
        share = geo.shares[which]
        return totals[which][pl.ds(pl.multiple_of(owner(slot) * share, CHUNK), share), :]

    def over_slots(low, high, body):
        lax.fori_loop(low, high, lambda slot, carry: (body(slot), carry)[1], 0)

    def rs_copy(which, stage, source, target, slot):
        return pltpu.make_async_remote_copy(
            src_ref=source,
            dst_ref=target,
            send_sem=rs_send.at[which, stage],
            recv_sem=rs_recv.at[which, stage],
            device_id=(owner(slot), core),
            device_id_type=MESH,
        )

    def rs_first(which):
        if not geo.scattered:
            return
        send_a, recv_a = staged[which][0:2]
        many = wide // 2

        def fill(slot):
            send_a[slot - many] = owned(which, slot).astype(BF16)

        over_slots(many, wide, fill)
        rs_copy(which, 0, send_a, recv_a, many).start()

    def rs_second(which):
        if not geo.scattered:
            return
        send_a, recv_a, send_b, recv_b = staged[which][0:4]
        rs_copy(which, 0, send_a, recv_a, wide // 2).wait_recv()
        many = wide // 4

        def fill(slot):
            send_b[slot - many] = (owned(which, slot) + recv_a[slot].astype(F32)).astype(BF16)

        over_slots(many, 2 * many, fill)
        rs_copy(which, 1, send_b, recv_b, many).start()

    def rs_third(which):
        if not geo.scattered:
            return
        _, recv_a, send_b, recv_b, send_c, recv_c = staged[which]
        rs_copy(which, 1, send_b, recv_b, wide // 4).wait_recv()

        def fill(slot):
            send_c[slot - 1] = (
                owned(which, slot) + recv_a[slot].astype(F32) + recv_b[slot].astype(F32)
            ).astype(BF16)
            rs_copy(which, 2, send_c.at[slot - 1], recv_c.at[slot - 1], slot).start()

        over_slots(1, wide // 4, fill)

    def rs_last(which):
        if not geo.scattered:
            store(totals[which], weight_outs[which])
            return
        _, recv_a, _, recv_b, _, recv_c = staged[which]
        pltpu.make_async_copy(recv_c, recv_c, rs_recv.at[which, 2]).wait()
        value = owned(which, 0) + recv_a[0].astype(F32) + recv_b[0].astype(F32)
        for index in range(wide // 4 - 1):
            value = value + recv_c[index].astype(F32)
        weight_stage[which][...] = value
        store(weight_stage[which], weight_outs[which])

    def rs_drain(which):
        if not geo.scattered:
            return
        for stage in range(3):
            source = staged[which][2 * stage]
            pltpu.make_async_copy(source, source, rs_send.at[which, stage]).wait()

    sums_three = get_sums(3)
    slopes(
        up_three, norm_three, slope_three, scale_three, gain_three, sums_three, inverse_wide, geo.wide_half
    )
    send_two[...] = dot_turned(slope_three[...], conv_last[span(other * half, half), :]).astype(BF16)
    copy_back_two = sibling(5, send_two, recv_two)
    copy_back_two.start()
    totals[0][...] = dot(turned_two[...], slope_three[...])
    rs_first(0)
    up_two[...] = dot_turned(slope_three[...], conv_last[span(core * half, half), :])
    give_affine(2, sums_three)
    copy_back_two.wait_recv()

    def back_sums(up, received, slope_act, normed):
        def step(rows, carry):
            value = (up[rows, :] + received[rows, :].astype(F32)) * slope_act[rows, :]
            up[rows, :] = value
            return carry[0] + fold_rows(value), carry[1] + fold_rows(value * normed[rows, :])

        zero = jnp.zeros((8, half), F32)
        return over_rows(step, (zero, zero))

    send_sums(4, *back_sums(up_two, recv_two, slope_act_two, norm_two))
    sums_two = get_sums(4)
    slopes(up_two, norm_two, slope_two, scale_two, gain_two, sums_two, inverse, half, shifted_src)

    def back_parts(low):
        for position in range(9):
            rows = pl.ds(pl.multiple_of(position * geo.hidden + low, half), half)
            parts[position, whole, :] = dot_turned(slope_two[...], conv_middle[rows, :])
        return fold_parts(lambda position: 8 - position)

    for group, value in enumerate(back_parts(other * half)):
        send_one[geo.starts[group] : geo.starts[group] + geo.padded[group], :] = value.astype(BF16)
    copy_back_one = sibling(6, send_one, recv_one)
    copy_back_one.start()
    for position in range(9):
        flipped = 8 - position
        for group in range(3):
            start, rows = geo.starts[group], geo.padded[group]
            value = gather_shifted(shifted_src, flipped, group)
            if position != 4:
                value = value * spread(shift_masks[flipped, start : start + rows, :], half)
            shifted[start : start + rows, :] = value.astype(BF16)
        totals[1][position * geo.hidden : (position + 1) * geo.hidden, :] = dot(
            turned_one[...], shifted[...]
        )
    rs_first(1)
    for group, value in enumerate(back_parts(core * half)):
        up_one[geo.starts[group] : geo.starts[group] + geo.padded[group], :] = value
    give_affine(1, sums_two)
    rs_second(0)
    copy_back_one.wait_recv()

    send_sums(5, *back_sums(up_one, recv_one, slope_act_one, norm_one))
    rs_third(0)
    sums_one = get_sums(5)
    slopes(up_one, norm_one, slope_one, scale_one, gain_one, sums_one, inverse, half)
    send_in[...] = dot_turned(
        slope_one[...], conv_first[span(other * geo.wide_half, geo.wide_half), :]
    ).astype(BF16)
    copy_in = sibling(7, send_in, recv_in)
    copy_in.start()
    totals[2][...] = dot(x_turned[...], slope_one[...])
    rs_first(2)
    rs_second(1)
    up_three[...] += dot_turned(slope_one[...], conv_first[span(core * geo.wide_half, geo.wide_half), :])
    give_affine(0, sums_one)
    copy_in.wait_recv()
    for group in range(3):
        start, real, rows = geo.starts[group], geo.real[group], geo.padded[group]
        value = up_three[start : start + rows, :] + recv_in[start : start + rows, :].astype(F32)
        value = value[0:real, :].reshape(geo.pixels[group], slots, geo.wide_half)
        raw_grad[group][...] = value.astype(BF16)
        store(raw_grad[group], in_grads[group])
    rs_last(0)
    rs_third(1)
    rs_second(2)
    rs_third(2)
    rs_last(1)
    rs_last(2)

    for copy in (*x_copies, copy_one, copy_two, copy_back_two, copy_back_one, copy_in):
        copy.wait_send()
    for round_index in range(6):
        stat_wait(round_index, stat_send)
    for which in range(3):
        rs_drain(which)
    for copy in stores:
        copy.wait()


def run_block(
    wide,
    live_counts,
    small_in,
    mid_in,
    big_in,
    conv_first,
    conv_middle,
    conv_last,
    gain_first,
    shift_first,
    gain_middle,
    shift_middle,
    gain_last,
    shift_last,
    small_cot,
    mid_cot,
    big_cot,
):
    maps = (small_in, mid_in, big_in)
    cots = (small_cot, mid_cot, big_cot)
    channels = 2 * small_in.shape[3]
    hidden, half = conv_last.shape[0], conv_first.shape[1]
    geo = Geometry(wide, [tensor.shape for tensor in maps], channels, hidden, half)
    across = geo.wide_half

    def as_rows(tensor):
        count, height, width, depth = tensor.shape
        return jnp.transpose(tensor, (1, 2, 0, 3)).reshape(height * width, count, depth)

    def as_maps(rows, like):
        count, height, width, depth = like.shape
        return jnp.transpose(rows.reshape(height, width, count, depth), (2, 0, 1, 3))

    affine = [
        vector.reshape(1, -1)
        for vector in (gain_first, shift_first, gain_middle, shift_middle, gain_last, shift_last)
    ]
    operands = [
        live_counts,
        *[as_rows(tensor) for tensor in maps],
        conv_first,
        conv_middle,
        conv_last,
        *affine,
        *[as_rows(tensor) for tensor in cots],
    ]
    raw_shapes = [(count, geo.slots, across) for count in geo.pixels]
    weight_shapes = [(hidden, across), (9 * hidden, half), (channels, half)]
    share_shapes = [
        (share, shape[1]) if geo.scattered else shape
        for share, shape in zip(geo.shares, weight_shapes)
    ]
    out_shapes = [jax.ShapeDtypeStruct(shape, BF16) for shape in raw_shapes * 2]
    out_shapes += [jax.ShapeDtypeStruct(shape, F32) for shape in share_shapes]
    out_shapes += [jax.ShapeDtypeStruct(vector.shape, F32) for vector in affine]

    def vmem(dtype, *shape):
        return pltpu.VMEM(shape, dtype)

    rows, guarded = geo.rows, geo.rows + 2 * GUARD
    scratch = [vmem(BF16, *shape) for shape in raw_shapes * 4]
    scratch += [vmem(BF16, *tensor.shape) for tensor in (conv_first, conv_middle, conv_last)]
    scratch += [vmem(F32, *vector.shape) for vector in affine]
    scratch += [vmem(F32, rows, LANES), vmem(F32, 9, rows, LANES)]
    scratch += [vmem(BF16, 2, rows, across), vmem(BF16, channels, rows), vmem(F32, rows, across)]
    scratch += [vmem(F32, rows, half), vmem(F32, rows, half), vmem(F32, rows, across)]
    scratch += [vmem(F32, rows, half)] * 2
    scratch += [vmem(BF16, 2, rows, half)] * 2 + [vmem(BF16, hidden, rows)] * 2
    scratch += [vmem(F32, 9, guarded, half), vmem(F32, guarded, half), vmem(BF16, rows, half)]
    scratch += [vmem(F32, rows, across)] * 2 + [vmem(F32, rows, half)] * 2
    scratch += [vmem(BF16, rows, across), vmem(BF16, rows, half), vmem(BF16, rows, half)]
    scratch += [vmem(BF16, rows, half)] * 4 + [vmem(BF16, rows, across)] * 2
    scratch += [
        vmem(F32, wide, 3, half),
        vmem(F32, wide, 2, half),
        vmem(F32, wide, 2, across),
        vmem(F32, wide, 2, across),
        vmem(F32, wide, 2, half),
        vmem(F32, wide, 2, half),
    ]
    scratch += [vmem(F32, *shape) for shape in weight_shapes]
    if geo.scattered:
        for share, shape in zip(geo.shares, weight_shapes):
            for many in (wide // 2, wide // 4, wide // 4 - 1):
                scratch += [vmem(BF16, many, share, shape[1])] * 2
    scratch += [vmem(F32, *shape) for shape in (share_shapes if geo.scattered else [(8, LANES)] * 3)]
    scratch += [vmem(F32, *vector.shape) for vector in affine]
    dma = pltpu.SemaphoreType.DMA
    scratch += [dma((18,)), dma((15,)), dma((8,)), dma((8,)), dma((6,)), dma((6,))]
    if geo.scattered:
        scratch += [dma((3, 3)), dma((3, 3))]

    anywhere = pl.BlockSpec(memory_space=pl.ANY)
    results = pl.pallas_call(
        functools.partial(block_kernel, geo),
        out_shape=out_shapes,
        in_specs=[pl.BlockSpec(memory_space=pltpu.SMEM)] + [anywhere] * (len(operands) - 1),
        out_specs=[anywhere] * len(out_shapes),
        scratch_shapes=scratch,
        compiler_params=pltpu.CompilerParams(
            collective_id=0, has_side_effects=True, vmem_limit_bytes=60 * 2**20
        ),
    )(*operands)
    images = [as_maps(rows, like) for rows, like in zip(results[0:6], maps * 2)]
    last_grad, middle_grad, first_grad = results[6:9]
    if not geo.scattered:
        first_grad, middle_grad, last_grad = (
            lax.psum_scatter(grad, "wide", scatter_dimension=0, tiled=True)
            for grad in (first_grad, middle_grad, last_grad)
        )
    vectors = [vector.reshape(-1) for vector in results[9:15]]
    return (*images, first_grad, middle_grad, last_grad, *vectors)


def solution(mesh):
    images = P("wide", None, None, "narrow")
    columns = P(None, "narrow")
    vector = P("narrow")
    return jax.shard_map(
        functools.partial(run_block, mesh.shape["wide"]),
        mesh=mesh,
        in_specs=(P("wide", None),) + (images,) * 3 + (columns,) * 3 + (vector,) * 6 + (images,) * 3,
        out_specs=(images,) * 6 + (P("wide", "narrow"),) * 3 + (vector,) * 6,
        check_vma=False,
    )
```

time: 922 us -> 122 us (0.13); the launches traced: 911 us -> 121 us
  blocking collectives: 374 us -> 0 us
  waiting for transfers between devices: 315 us -> 0 us
  other arithmetic: 109 us -> 0 us
  Pallas kernels: 0 us -> 106 us
  local copies, waits for them, and re-layouts: 57.4 us -> 14.1 us
  matrix products: 37 us -> 0 us
  between operations: 18 us -> 0.76 us
    psum x9 -> x0, blocking collectives: 354 us -> none  [the longest x3 123 us: norm_back(): lax.psum((channel_sum(upstream, masks), channel_sum(crossed, masks)), 'wi...]
    reduce_scatter x12 -> x0, waiting for transfers between devices: 315 us -> none  [the longest x1 141 us: local(): lax.psum_scatter(middle_grad, 'wide', scatter_dimension=0, tiled=True)]
    pallas_call x0 -> x1, Pallas kernels: none -> 106 us  [run_block(): pl.pallas_call(functools.partial(block_kernel, geo), out_shape=out_shapes...]
    dot_general x27 -> x0, matrix products: 37 us -> none  [the longest x9 14.5 us: project(): jnp.dot(tensor.reshape(-1, tensor.shape[-1]), weight, preferred_element_t...]
    convert_element_type x20 -> x0, other arithmetic: 33.3 us -> none  [the longest x9 15.2 us: norm_back(): (part_mask * factor * (grad - total_grad / count - value * total_cross /...]
    scatter-add x27 -> x0, local copies, waits for them, and re-layouts: 33.1 us -> none  [fold_patches(): padded.at[:, offset_y:offset_y + height, offset_x:offset_x + width, :]]
    reduce_sum x20 -> x0, other arithmetic: 31.2 us -> none  [the longest x18 28.1 us: channel_sum(): jnp.sum(tensor * part_mask, axis=(0, 1, 2))]
    add x33 -> x0, other arithmetic: 27.9 us -> none  [the longest x21 27.9 us: fold_patches(): padded.at[:, offset_y:offset_y + height, offset_x:offset_x + width, :]]
  transfers between devices with their start and end apart: 12 -> 0, of which waited for: 5 -> 0; matrix products, arithmetic and copies ran while one was open for 10% -> 0% of each run, Pallas kernels for 0% -> 0%
where the time goes in v1:
time: 122 us; the launch traced here: 121 us
  Pallas kernels  106 us (87%)
  local copies, waits for them, and re-layouts  14.1 us (12%)
    pallas_call x1, Pallas kernels, run_block(): pl.pallas_call(functools.partial(block_kernel, geo), out_shape=out_shapes...  106 us
    unnamed x37, local copies, waits for them, and re-layouts  14.1 us

profile of v1, /device:TPU:0, one launch (start us, length us, event | category | flops | bytes accessed | tf_op | source)
XLA Modules:
  0.0 121.3 jit_solution(13039123714971084390)
XLA Ops:
  0.7 106.4 %shard_map.271 = (bf16[25,4,1024]{2,1,0:T(4,128)(2,1)}, bf16[36,4,1024]{2,1,0:T(4,128)(2,1)}, bf16[49,4,1024]{2,1,0:T(4,128)(2,1)}, bf16[25,4,1024]{2,1,0:T(4,12...) custom-call(s32[1,3]{1,0:T(1,128)} %refs_0_.1, ...), custom_call_target="tpu_custom_call" | custom-call | tf_op jit(solution)/shard_map/pallas_call | solution.py:683
  107.1 0.0 copy-start.2
  107.1 0.0 copy-start
  107.1 0.0 copy-start.4
  107.1 0.0 copy-start.1
  107.1 0.0 copy-start.3
  107.2 1.8 %copy.46 = bf16[4,5,5,1024]{3,0,2,1:T(4,128)(2,1)} copy(bf16[4,5,5,1024]{3,0,2,1:T(4,128)(2,1)} %bitcast.57) | data formatting | bytes 409600
  109.0 1.8 %copy.47 = bf16[4,6,6,1024]{3,0,2,1:T(4,128)(2,1)} copy(bf16[4,6,6,1024]{3,0,2,1:T(4,128)(2,1)} %bitcast.55) | data formatting | bytes 589824
  110.7 1.9 %copy.48 = bf16[4,7,7,1024]{3,0,2,1:T(4,128)(2,1)} copy(bf16[4,7,7,1024]{3,0,2,1:T(4,128)(2,1)} %bitcast.51) | data formatting | bytes 802816
  112.6 1.7 %copy.49 = bf16[4,5,5,1024]{3,0,2,1:T(4,128)(2,1)} copy(bf16[4,5,5,1024]{3,0,2,1:T(4,128)(2,1)} %bitcast.56) | data formatting | bytes 409600
  114.3 0.7 copy.50
  115.0 0.7 copy.51
  115.8 0.7 copy.52
  116.4 0.7 copy.53
  117.2 0.0 copy-done.3
  117.2 0.7 copy.54
  117.8 0.0 copy-done.10
  117.8 0.6 copy.55
  118.4 0.6 copy.56
  118.9 0.6 copy.57
  119.5 0.6 copy.58
  120.1 0.0 copy-done.6
  120.1 0.6 copy.59
  120.7 0.6 copy.60
  (14 shorter events, 0.0 us)
Async XLA Ops:
  107.1 7.2 %copy-start.2 = (bf16[36,4,1024]{2,1,0:T(4,128)(2,1)S(1)}, bf16[36,4,1024]{2,1,0:T(4,128)(2,1)}, u32[]{:S(2)}) copy-start(bf16[36,4,1024]{2,1,0:T(4,128)(2,1)} %get-tuple-element.34) | copy-start | bytes 884740
  107.1 7.9 %copy-start = (bf16[49,4,1024]{2,1,0:T(4,128)(2,1)S(1)}, bf16[49,4,1024]{2,1,0:T(4,128)(2,1)}, u32[]{:S(2)}) copy-start(bf16[49,4,1024]{2,1,0:T(4,128)(2,1)} %get-tuple-element.35) | copy-start | bytes 1204228
  107.1 8.7 %copy-start.4 = (f32[128,256]{1,0:T(8,128)S(1)}, f32[128,256]{1,0:T(8,128)}, u32[]{:S(2)}) copy-start(f32[128,256]{1,0:T(8,128)} %get-tuple-element.66) | copy-start | bytes 393220
  107.1 9.3 %copy-start.1 = (f32[288,256]{1,0:T(8,128)S(1)}, f32[288,256]{1,0:T(8,128)}, u32[]{:S(2)}) copy-start(f32[288,256]{1,0:T(8,128)} %get-tuple-element.67) | copy-start | bytes 884740
  107.1 10.0 %copy-start.3 = (f32[32,1024]{1,0:T(8,128)S(1)}, f32[32,1024]{1,0:T(8,128)}, u32[]{:S(2)}) copy-start(f32[32,1024]{1,0:T(8,128)} %get-tuple-element.68) | copy-start | bytes 393220
  107.1 10.7 %copy-start.10 = (f32[1,256]{1,0:T(1,128)S(1)}, f32[1,256]{1,0:T(1,128)}, u32[]{:S(2)}) copy-start(f32[1,256]{1,0:T(1,128)} %get-tuple-element.39) | copy-start | bytes 3076
  107.1 11.2 %copy-start.9 = (f32[1,256]{1,0:T(1,128)S(1)}, f32[1,256]{1,0:T(1,128)}, u32[]{:S(2)}) copy-start(f32[1,256]{1,0:T(1,128)} %get-tuple-element.40) | copy-start | bytes 3076
  107.2 11.8 %copy-start.8 = (f32[1,256]{1,0:T(1,128)S(1)}, f32[1,256]{1,0:T(1,128)}, u32[]{:S(2)}) copy-start(f32[1,256]{1,0:T(1,128)} %get-tuple-element.41) | copy-start | bytes 3076
  107.2 12.3 %copy-start.7 = (f32[1,256]{1,0:T(1,128)S(1)}, f32[1,256]{1,0:T(1,128)}, u32[]{:S(2)}) copy-start(f32[1,256]{1,0:T(1,128)} %get-tuple-element.42) | copy-start | bytes 3076
  107.2 12.9 %copy-start.6 = (f32[1,1024]{1,0:T(1,128)S(1)}, f32[1,1024]{1,0:T(1,128)}, u32[]{:S(2)}) copy-start(f32[1,1024]{1,0:T(1,128)} %get-tuple-element.43) | copy-start | bytes 12292
  107.2 13.5 %copy-start.5 = (f32[1,1024]{1,0:T(1,128)S(1)}, f32[1,1024]{1,0:T(1,128)}, u32[]{:S(2)}) copy-start(f32[1,1024]{1,0:T(1,128)} %get-tuple-element.44) | copy-start | bytes 12292

commit v2 on v1

--- a/solution.py
+++ b/solution.py
@@ -39,7 +39,11 @@
         bits = wide.bit_length() - 1
         self.bits = bits
         self.scattered = (
-            wide >= 8 and wide == 1 << bits and all(share % CHUNK == 0 for share in self.shares)
+            wide >= 8
+            and wide == 1 << bits
+            and all(share % CHUNK == 0 for share in self.shares)
+            and self.shares[2] % LANES == 0
+            and self.wide_half % self.shares[2] == 0
         )
 
 
@@ -82,7 +86,7 @@
     conv_first, conv_middle, conv_last = take(3)
     affine = take(6)
     live, shift_masks = take(2)
-    x_all, x_turned, cot_rows = take(3)
+    x_all, x_kept, x_given, cot_rows = take(4)
     norm_one, norm_two, norm_three = take(3)
     slope_act_one, slope_act_two = take(2)
     hidden_one, hidden_two, turned_one, turned_two = take(4)
@@ -92,11 +96,17 @@
     send_two, recv_two, send_one, recv_one, send_in, recv_in = take(6)
     stat_bufs = take(6)
     totals = take(3)
-    staged = [take(6) for _ in range(3)] if geo.scattered else None
+    if geo.scattered:
+        norm_one_half, norm_two_half, up_two_half, up_one_half, pair_slope = take(5)
+        pair_live, pair_norm_one, pair_norm_two, pair_up_two, pair_up_one = take(5)
+        pair_turned, pair_x, pair_src, live_half = take(4)
+        send_a, recv_a = take(2)
+        staged = [take(4) for _ in range(3)]
     weight_stage = take(3)
     affine_stage = take(6)
     load_sem, out_sem, sib_send, sib_recv, stat_send, stat_recv = take(6)
-    rs_send, rs_recv = take(2) if geo.scattered else (None, None)
+    if geo.scattered:
+        rs_send, rs_recv, pair_send, pair_recv = take(4)
     assert not refs
 
     wide, slots, half = geo.wide, geo.slots, geo.half
@@ -104,11 +114,21 @@
     core = lax.axis_index("narrow")
     other = 1 - core
 
-    loads = {}
+    pending = {}
+
+    def settle(*keys):
+        for key in keys:
+            pending.pop(key)()
+
+    def settle_all():
+        settle(*list(pending))
+
+    load_count = iter(range(18))
 
     def load(name, source, target):
-        loads[name] = pltpu.make_async_copy(source, target, load_sem.at[len(loads)])
-        loads[name].start()
+        copy = pltpu.make_async_copy(source, target, load_sem.at[next(load_count)])
+        copy.start()
+        pending[name] = copy.wait
 
     for group in range(3):
         load(("x", group), inputs[group], raw_x[group])
@@ -139,6 +159,8 @@
         image = index % slots
         mask = jnp.where((index < geo.real[group]) & (image < limit), 1.0, 0.0)
         live[geo.starts[group] : geo.starts[group] + rows, :] = mask
+        if geo.scattered:
+            live_half[geo.starts[group] : geo.starts[group] + rows, :] = mask.astype(BF16)
     count_here = jnp.full((1, LANES), local_count, jnp.int32).astype(F32)
 
     shift_masks[...] = jnp.ones_like(shift_masks)
@@ -161,8 +183,9 @@
         for position in range(9):
             buffer[position, 0:GUARD, :] = jnp.zeros((GUARD, half), F32)
             buffer[position, GUARD + geo.rows :, :] = jnp.zeros((GUARD, half), F32)
-    shifted_src[0:GUARD, :] = jnp.zeros((GUARD, half), F32)
-    shifted_src[GUARD + geo.rows :, :] = jnp.zeros((GUARD, half), F32)
+    for buffer in (shifted_src, pair_src) if geo.scattered else (shifted_src,):
+        buffer[0:GUARD, :] = jnp.zeros((GUARD, half), F32)
+        buffer[GUARD + geo.rows :, :] = jnp.zeros((GUARD, half), F32)
 
     def spread(tile, width):
         return jnp.concatenate([tile] * (width // LANES), axis=1)
@@ -181,17 +204,53 @@
     def column_sum(value):
         return jnp.sum(value, axis=0, keepdims=True)
 
+    def weigh(stage):
+        if stage == 0:
+            return 1 + core
+        if stage == 1:
+            return 2 - core
+        return 1 << stage
+
+    def owner(slot):
+        place = me
+        for stage in range(geo.bits):
+            chosen = (slot // (1 << (geo.bits - 1 - stage))) % 2
+            weight = weigh(stage)
+            mine = (me // weight) % 2
+            place = place + chosen * (1 - 2 * mine) * weight
+        return place
+
+    def over_slots(low, high, body):
+        lax.fori_loop(low, high, lambda slot, carry: (body(slot), carry)[1], 0)
+
+    def to_pair(name, index, source, target):
+        if not geo.scattered:
+            return
+        copy = pltpu.make_async_remote_copy(
+            src_ref=source,
+            dst_ref=target,
+            send_sem=pair_send.at[index],
+            recv_sem=pair_recv.at[index],
+            device_id=(owner(wide // 2), core),
+            device_id_type=MESH,
+        )
+        copy.start()
+        pending["pair", name] = copy.wait_recv
+        pending["pair sent", name] = copy.wait_send
+
     to_other = {"device_id": (me, other), "device_id_type": MESH}
 
-    def sibling(index, source, target):
-        return pltpu.make_async_remote_copy(
+    def exchange(name, index, source, target):
+        copy = pltpu.make_async_remote_copy(
             src_ref=source, dst_ref=target, send_sem=sib_send.at[index], recv_sem=sib_recv.at[index], **to_other
         )
-
-    x_copies = []
-    pl_wait_done = False
+        copy.start()
+        pending[name] = copy.wait_recv
+        pending[name, "sent"] = copy.wait_send
+
+    greeted = False
     for group in range(3):
-        loads[("x", group)].wait()
+        settle(("x", group))
         rows, real, start = geo.padded[group], geo.real[group], geo.starts[group]
         value = raw_x[group][...].astype(F32).reshape(real, geo.wide_half)
         if rows > real:
@@ -199,17 +258,14 @@
         mask = spread(live[start : start + rows, :], geo.wide_half)
         place = x_all.at[core, pl.ds(start, rows)]
         place[...] = (value * mask).astype(BF16)
-        if not pl_wait_done:
+        if not greeted:
             pl.semaphore_wait(barrier, wide)
-            pl_wait_done = True
-        copy = sibling(group, place, place)
-        copy.start()
-        x_copies.append(copy)
-
-    loads["first"].wait()
+            greeted = True
+        exchange(("x other", group), group, place, place)
+
+    settle("first")
     norm_one[...] = dot(x_all[core], conv_first[span(core * geo.wide_half, geo.wide_half), :])
-    for copy in x_copies:
-        copy.wait_recv()
+    settle(*(("x other", group) for group in range(3)))
     norm_one[...] += dot(x_all[other], conv_first[span(other * geo.wide_half, geo.wide_half), :])
 
     def broadcast(round_index):
@@ -228,10 +284,9 @@
             return carry
 
         lax.fori_loop(0, wide - 1, push, 0)
-
-    def stat_wait(round_index, sem):
-        view = stat_bufs[round_index].at[pl.ds(0, wide - 1)]
-        pltpu.make_async_copy(view, view, sem.at[round_index]).wait()
+        view = buffer.at[pl.ds(0, wide - 1)]
+        pending["stat", round_index] = pltpu.make_async_copy(view, view, stat_recv.at[round_index]).wait
+        pending["stat sent", round_index] = pltpu.make_async_copy(view, view, stat_send.at[round_index]).wait
 
     def send_moments(round_index, values, width):
         def add(rows, carry):
@@ -256,7 +311,7 @@
         return [spread(stat_bufs[0][index, 2:3, 0:LANES], width) for index in range(wide)]
 
     def get_moments(round_index, width):
-        stat_wait(round_index, stat_recv)
+        settle(("stat", round_index))
         buffer = stat_bufs[round_index]
         each = counts(width)
         total_count = sum(each)
@@ -274,16 +329,18 @@
         broadcast(round_index)
 
     def get_sums(round_index):
-        stat_wait(round_index, stat_recv)
+        settle(("stat", round_index))
         buffer = stat_bufs[round_index]
         total = sum(buffer[index] for index in range(wide))
         return total[0:1, :], total[1:2, :]
 
-    def activate(values, slope_act, hidden, centre, scale, gain, shift):
+    def activate(values, halved, slope_act, hidden, centre, scale, gain, shift):
         def step(rows, carry):
             mask = live_rows(rows, half)
             normed = (values[rows, :] - centre) * scale
             values[rows, :] = normed
+            if halved is not None:
+                halved[rows, :] = normed.astype(BF16)
             act = normed * gain + shift
             share, slope = gelu_parts(act)
             hidden[core, rows, :] = (act * share * mask).astype(BF16)
@@ -312,17 +369,32 @@
         return results
 
     send_moments(0, norm_one, half)
-    for index in range(2):
-        x_turned[index * geo.wide_half : (index + 1) * geo.wide_half, :] = x_all[index].T
+    if geo.scattered:
+        share = geo.shares[2]
+        per_half = geo.wide_half // share
+
+        def turn(place, slot, target):
+            low = pl.multiple_of((place % per_half) * share, share)
+            target[slot] = x_all[place // per_half, :, pl.ds(low, share)].T
+
+        many, part = wide // 2, wide // 4
+        over_slots(many, many + part, lambda slot: turn(owner(slot), slot - many, x_given))
+        low, high = pl.ds(0, part), pl.ds(part, part)
+        to_pair("x low", 1, x_given.at[low], pair_x.at[low])
+        to_pair("live", 0, live_half, pair_live)
+        over_slots(many + part, wide, lambda slot: turn(owner(slot), slot - many, x_given))
+        over_slots(0, many, lambda slot: turn(owner(slot), slot, x_kept))
+    else:
+        for index in range(2):
+            x_kept[index * geo.wide_half : (index + 1) * geo.wide_half, :] = x_all[index].T
     for index in range(6):
-        loads[("affine", index)].wait()
+        settle(("affine", index))
     gain_one, shift_one, gain_two, shift_two, gain_three, shift_three = (ref[...] for ref in affine)
     centre_one, scale_one, inverse = get_moments(0, half)
-    activate(norm_one, slope_act_one, hidden_one, centre_one, scale_one, gain_one, shift_one)
-    copy_one = sibling(3, hidden_one.at[core], hidden_one.at[core])
-    copy_one.start()
-    loads["middle"].wait()
-    copy_one.wait_recv()
+    half_one, half_two = (norm_one_half, norm_two_half) if geo.scattered else (None, None)
+    activate(norm_one, half_one, slope_act_one, hidden_one, centre_one, scale_one, gain_one, shift_one)
+    exchange("hidden one", 3, hidden_one.at[core], hidden_one.at[core])
+    settle("middle", "hidden one")
 
     whole = slice(GUARD, GUARD + geo.rows)
     for position in range(9):
@@ -333,23 +405,25 @@
     for group, value in enumerate(fold_parts(lambda position: position)):
         norm_two[geo.starts[group] : geo.starts[group] + geo.padded[group], :] = value
     send_moments(1, norm_two, half)
+    if geo.scattered:
+        to_pair("x high", 7, x_given.at[high], pair_x.at[high])
     for index in range(2):
         turned_one[index * half : (index + 1) * half, :] = hidden_one[index].T
     for group in range(3):
-        loads[("cot", group)].wait()
+        settle(("cot", group))
         rows, real, start = geo.padded[group], geo.real[group], geo.starts[group]
         value = raw_cot[group][...].astype(F32).reshape(real, geo.wide_half)
         if rows > real:
             value = jnp.concatenate([value, jnp.zeros((rows - real, geo.wide_half), F32)], axis=0)
         cot_rows[start : start + rows, :] = value * spread(live[start : start + rows, :], geo.wide_half)
     centre_two, scale_two, _ = get_moments(1, half)
-    activate(norm_two, slope_act_two, hidden_two, centre_two, scale_two, gain_two, shift_two)
-    copy_two = sibling(4, hidden_two.at[core], hidden_two.at[core])
-    copy_two.start()
-    loads["last"].wait()
-    copy_two.wait_recv()
+    activate(norm_two, half_two, slope_act_two, hidden_two, centre_two, scale_two, gain_two, shift_two)
+    exchange("hidden two", 4, hidden_two.at[core], hidden_two.at[core])
+    settle("last", "hidden two")
     norm_three[...] = dot(hidden_two[0], conv_last[0:half, :]) + dot(hidden_two[1], conv_last[half:, :])
     send_moments(2, norm_three, geo.wide_half)
+    if geo.scattered:
+        to_pair("turned", 3, turned_one, pair_turned)
     for index in range(2):
         turned_two[index * half : (index + 1) * half, :] = hidden_two[index].T
     centre_three, scale_three, inverse_wide = get_moments(2, geo.wide_half)
@@ -367,13 +441,17 @@
 
     zero_wide = jnp.zeros((8, geo.wide_half), F32)
     send_sums(3, *over_rows(finish, (zero_wide, zero_wide)))
-
-    stores = []
+    if geo.scattered:
+        to_pair("norm two", 4, norm_two_half, pair_norm_two)
+        to_pair("norm one", 2, norm_one_half, pair_norm_one)
+
+    store_count = iter(range(15))
 
     def store(source, target):
-        copy = pltpu.make_async_copy(source, target, out_sem.at[len(stores)])
+        index = next(store_count)
+        copy = pltpu.make_async_copy(source, target, out_sem.at[index])
         copy.start()
-        stores.append(copy)
+        pending["store", index] = copy.wait
 
     for group in range(3):
         start, real = geo.starts[group], geo.real[group]
@@ -381,16 +459,16 @@
         raw_out[group][...] = value.astype(BF16)
         store(raw_out[group], outs[group])
 
-    def slopes(up, normed, target, scale, gain, sums, inverse_count, width, plain=None):
+    def slopes(up, normed, mask, target, scale, gain, sums, inverse_count, width, plain=None):
         grad_total, cross_total = sums
         factor = gain * scale
         grad_mean, cross_mean = grad_total * inverse_count, cross_total * inverse_count
 
         def step(rows, carry):
-            value = live_rows(rows, width) * (
-                factor * (up[rows, :] - grad_mean - normed[rows, :] * cross_mean)
-            )
-            target[rows, :] = value.astype(BF16)
+            gap = up[rows, :].astype(F32) - grad_mean - normed[rows, :].astype(F32) * cross_mean
+            value = spread(mask[rows, :].astype(F32), width) * (factor * gap)
+            if target is not None:
+                target[rows, :] = value.astype(BF16)
             if plain is not None:
                 plain[pl.ds(pl.multiple_of(GUARD + rows.start, CHUNK), CHUNK), :] = value
             return carry
@@ -403,122 +481,115 @@
         for place in (2 * index, 2 * index + 1):
             store(affine_stage[place], affine_outs[place])
 
-    def weigh(stage):
-        if stage == 0:
-            return 1 + core
-        if stage == 1:
-            return 2 - core
-        return 1 << stage
-
-    def owner(slot):
-        place = me
-        for stage in range(geo.bits):
-            chosen = (slot // (1 << (geo.bits - 1 - stage))) % 2
-            weight = weigh(stage)
-            mine = (me // weight) % 2
-            place = place + chosen * (1 - 2 * mine) * weight
-        return place
-
     def owned(which, slot):
+        if which == 2:
+            return totals[2][slot]
         share = geo.shares[which]
         return totals[which][pl.ds(pl.multiple_of(owner(slot) * share, CHUNK), share), :]
 
-    def over_slots(low, high, body):
-        lax.fori_loop(low, high, lambda slot, carry: (body(slot), carry)[1], 0)
-
-    def rs_copy(which, stage, source, target, slot):
-        return pltpu.make_async_remote_copy(
+    def reduced(which, slot):
+        value = owned(which, slot)
+        return value + recv_a[slot].astype(F32) if which == 0 else value
+
+    quarter = wide // 4
+
+    def rs_start(which, stage, piece, source, target, slot):
+        copy = pltpu.make_async_remote_copy(
             src_ref=source,
             dst_ref=target,
-            send_sem=rs_send.at[which, stage],
-            recv_sem=rs_recv.at[which, stage],
+            send_sem=rs_send.at[which, stage, piece],
+            recv_sem=rs_recv.at[which, stage, piece],
             device_id=(owner(slot), core),
             device_id_type=MESH,
         )
-
-    def rs_first(which):
-        if not geo.scattered:
-            return
-        send_a, recv_a = staged[which][0:2]
-        many = wide // 2
-
-        def fill(slot):
-            send_a[slot - many] = owned(which, slot).astype(BF16)
-
-        over_slots(many, wide, fill)
-        rs_copy(which, 0, send_a, recv_a, many).start()
+        copy.start()
+        pending["scatter", which, stage, piece] = copy.wait_recv
+        pending["scatter sent", which, stage, piece] = copy.wait_send
+
+    def rs_first():
+        for piece in (1, 0):
+            low = piece * quarter
+
+            def fill(slot):
+                send_a[slot] = owned(0, slot + wide // 2).astype(BF16)
+
+            over_slots(low, low + quarter, fill)
+            part = pl.ds(low, quarter)
+            rs_start(0, 0, piece, send_a.at[part], recv_a.at[part], wide // 2)
 
     def rs_second(which):
-        if not geo.scattered:
-            return
-        send_a, recv_a, send_b, recv_b = staged[which][0:4]
-        rs_copy(which, 0, send_a, recv_a, wide // 2).wait_recv()
-        many = wide // 4
-
-        def fill(slot):
-            send_b[slot - many] = (owned(which, slot) + recv_a[slot].astype(F32)).astype(BF16)
-
-        over_slots(many, 2 * many, fill)
-        rs_copy(which, 1, send_b, recv_b, many).start()
+        send_b, recv_b = staged[which][0:2]
+        if which == 0:
+            settle(("scatter", 0, 0, 1))
+        for slot in reversed(range(quarter)):
+            send_b[slot] = reduced(which, slot + quarter).astype(BF16)
+            rs_start(which, 1, slot, send_b.at[slot], recv_b.at[slot], quarter)
 
     def rs_third(which):
-        if not geo.scattered:
-            return
-        _, recv_a, send_b, recv_b, send_c, recv_c = staged[which]
-        rs_copy(which, 1, send_b, recv_b, wide // 4).wait_recv()
-
-        def fill(slot):
-            send_c[slot - 1] = (
-                owned(which, slot) + recv_a[slot].astype(F32) + recv_b[slot].astype(F32)
-            ).astype(BF16)
-            rs_copy(which, 2, send_c.at[slot - 1], recv_c.at[slot - 1], slot).start()
-
-        over_slots(1, wide // 4, fill)
+        _, recv_b, send_c, recv_c = staged[which]
+        if which == 0:
+            settle(("scatter", 0, 0, 0))
+        for slot in reversed(range(1, quarter)):
+            settle(("scatter", which, 1, slot))
+            send_c[slot - 1] = (reduced(which, slot) + recv_b[slot].astype(F32)).astype(BF16)
+            rs_start(which, 2, slot, send_c.at[slot - 1], recv_c.at[slot - 1], slot)
 
     def rs_last(which):
-        if not geo.scattered:
-            store(totals[which], weight_outs[which])
-            return
-        _, recv_a, _, recv_b, _, recv_c = staged[which]
-        pltpu.make_async_copy(recv_c, recv_c, rs_recv.at[which, 2]).wait()
-        value = owned(which, 0) + recv_a[0].astype(F32) + recv_b[0].astype(F32)
-        for index in range(wide // 4 - 1):
-            value = value + recv_c[index].astype(F32)
+        _, recv_b, _, recv_c = staged[which]
+        settle(("scatter", which, 1, 0))
+        value = reduced(which, 0) + recv_b[0].astype(F32)
+        for slot in range(1, quarter):
+            settle(("scatter", which, 2, slot))
+            value = value + recv_c[slot - 1].astype(F32)
         weight_stage[which][...] = value
         store(weight_stage[which], weight_outs[which])
 
-    def rs_drain(which):
-        if not geo.scattered:
-            return
-        for stage in range(3):
-            source = staged[which][2 * stage]
-            pltpu.make_async_copy(source, source, rs_send.at[which, stage]).wait()
-
     sums_three = get_sums(3)
     slopes(
-        up_three, norm_three, slope_three, scale_three, gain_three, sums_three, inverse_wide, geo.wide_half
+        up_three, norm_three, live, slope_three, scale_three, gain_three, sums_three, inverse_wide, geo.wide_half
     )
     send_two[...] = dot_turned(slope_three[...], conv_last[span(other * half, half), :]).astype(BF16)
-    copy_back_two = sibling(5, send_two, recv_two)
-    copy_back_two.start()
+    exchange("back two", 5, send_two, recv_two)
     totals[0][...] = dot(turned_two[...], slope_three[...])
-    rs_first(0)
+    if not geo.scattered:
+        store(totals[0], weight_outs[0])
     up_two[...] = dot_turned(slope_three[...], conv_last[span(core * half, half), :])
     give_affine(2, sums_three)
-    copy_back_two.wait_recv()
-
-    def back_sums(up, received, slope_act, normed):
+    settle("back two")
+
+    def back_sums(up, halved, received, slope_act, normed):
         def step(rows, carry):
             value = (up[rows, :] + received[rows, :].astype(F32)) * slope_act[rows, :]
             up[rows, :] = value
+            if halved is not None:
+                halved[rows, :] = value.astype(BF16)
             return carry[0] + fold_rows(value), carry[1] + fold_rows(value * normed[rows, :])
 
         zero = jnp.zeros((8, half), F32)
         return over_rows(step, (zero, zero))
 
-    send_sums(4, *back_sums(up_two, recv_two, slope_act_two, norm_two))
+    half_up_two, half_up_one = (up_two_half, up_one_half) if geo.scattered else (None, None)
+    send_sums(4, *back_sums(up_two, half_up_two, recv_two, slope_act_two, norm_two))
+    if geo.scattered:
+        to_pair("up two", 5, up_two_half, pair_up_two)
+        rs_first()
+        settle(("pair", "live"), ("pair", "norm two"), ("pair", "turned"))
     sums_two = get_sums(4)
-    slopes(up_two, norm_two, slope_two, scale_two, gain_two, sums_two, inverse, half, shifted_src)
+    slopes(up_two, norm_two, live, slope_two, scale_two, gain_two, sums_two, inverse, half, shifted_src)
+    if geo.scattered:
+        settle(("pair", "up two"))
+        slopes(
+            pair_up_two, pair_norm_two, pair_live, None, scale_two, gain_two, sums_two, inverse, half, pair_src
+        )
+
+    def shift_into(source, position):
+        flipped = 8 - position
+        for group in range(3):
+            start, rows = geo.starts[group], geo.padded[group]
+            value = gather_shifted(source, flipped, group)
+            if position != 4:
+                value = value * spread(shift_masks[flipped, start : start + rows, :], half)
+            shifted[start : start + rows, :] = value.astype(BF16)
 
     def back_parts(low):
         for position in range(9):
@@ -528,62 +599,79 @@
 
     for group, value in enumerate(back_parts(other * half)):
         send_one[geo.starts[group] : geo.starts[group] + geo.padded[group], :] = value.astype(BF16)
-    copy_back_one = sibling(6, send_one, recv_one)
-    copy_back_one.start()
-    for position in range(9):
-        flipped = 8 - position
-        for group in range(3):
-            start, rows = geo.starts[group], geo.padded[group]
-            value = gather_shifted(shifted_src, flipped, group)
-            if position != 4:
-                value = value * spread(shift_masks[flipped, start : start + rows, :], half)
-            shifted[start : start + rows, :] = value.astype(BF16)
-        totals[1][position * geo.hidden : (position + 1) * geo.hidden, :] = dot(
-            turned_one[...], shifted[...]
-        )
-    rs_first(1)
+    exchange("back one", 6, send_one, recv_one)
     for group, value in enumerate(back_parts(core * half)):
         up_one[geo.starts[group] : geo.starts[group] + geo.padded[group], :] = value
     give_affine(1, sums_two)
-    rs_second(0)
-    copy_back_one.wait_recv()
-
-    send_sums(5, *back_sums(up_one, recv_one, slope_act_one, norm_one))
-    rs_third(0)
+    settle("back one")
+
+    send_sums(5, *back_sums(up_one, half_up_one, recv_one, slope_act_one, norm_one))
+    if geo.scattered:
+        to_pair("up one", 6, up_one_half, pair_up_one)
+        rs_second(0)
+    for position in range(9):
+        place = slice(position * geo.hidden, (position + 1) * geo.hidden)
+        shift_into(shifted_src, position)
+        value = dot(turned_one[...], shifted[...])
+        if geo.scattered:
+            shift_into(pair_src, position)
+            value = value + dot(pair_turned[...], shifted[...])
+        totals[1][place, :] = value
+    if geo.scattered:
+        rs_second(1)
+        rs_third(0)
+        settle(("pair", "norm one"), ("pair", "x low"), ("pair", "x high"))
+    else:
+        store(totals[1], weight_outs[1])
     sums_one = get_sums(5)
-    slopes(up_one, norm_one, slope_one, scale_one, gain_one, sums_one, inverse, half)
+    slopes(up_one, norm_one, live, slope_one, scale_one, gain_one, sums_one, inverse, half)
+    if geo.scattered:
+        settle(("pair", "up one"))
+        slopes(
+            pair_up_one, pair_norm_one, pair_live, pair_slope, scale_one, gain_one, sums_one, inverse, half
+        )
+        share = geo.shares[2]
+        for slot in reversed(range(wide // 2)):
+            totals[2][slot] = dot(x_kept[slot], slope_one[...]) + dot(pair_x[slot], pair_slope[...])
+        rs_second(2)
+    else:
+        totals[2][...] = dot(x_kept[...], slope_one[...])
+        store(totals[2], weight_outs[2])
     send_in[...] = dot_turned(
         slope_one[...], conv_first[span(other * geo.wide_half, geo.wide_half), :]
     ).astype(BF16)
-    copy_in = sibling(7, send_in, recv_in)
-    copy_in.start()
-    totals[2][...] = dot(x_turned[...], slope_one[...])
-    rs_first(2)
-    rs_second(1)
+    exchange("back in", 7, send_in, recv_in)
+    if geo.scattered:
+        rs_third(1)
     up_three[...] += dot_turned(slope_one[...], conv_first[span(core * geo.wide_half, geo.wide_half), :])
     give_affine(0, sums_one)
-    copy_in.wait_recv()
+    settle("back in")
     for group in range(3):
         start, real, rows = geo.starts[group], geo.real[group], geo.padded[group]
         value = up_three[start : start + rows, :] + recv_in[start : start + rows, :].astype(F32)
         value = value[0:real, :].reshape(geo.pixels[group], slots, geo.wide_half)
         raw_grad[group][...] = value.astype(BF16)
         store(raw_grad[group], in_grads[group])
-    rs_last(0)
-    rs_third(1)
-    rs_second(2)
-    rs_third(2)
-    rs_last(1)
-    rs_last(2)
-
-    for copy in (*x_copies, copy_one, copy_two, copy_back_two, copy_back_one, copy_in):
-        copy.wait_send()
-    for round_index in range(6):
-        stat_wait(round_index, stat_send)
-    for which in range(3):
-        rs_drain(which)
-    for copy in stores:
-        copy.wait()
+    if geo.scattered:
+        rs_third(2)
+        rs_last(0)
+        rs_last(1)
+        rs_last(2)
+    settle_all()
+
+
+def copy_kernel(count, *refs):
+    sources, targets = refs[:count], refs[count : 2 * count]
+    held, sem = refs[2 * count : 3 * count], refs[3 * count]
+    loads = [pltpu.make_async_copy(sources[i], held[i], sem.at[0, i]) for i in range(count)]
+    stores = [pltpu.make_async_copy(held[i], targets[i], sem.at[1, i]) for i in range(count)]
+    for load in loads:
+        load.start()
+    for load, store in zip(loads, stores):
+        load.wait()
+        store.start()
+    for store in stores:
+        store.wait()
 
 
 def run_block(
@@ -651,7 +739,12 @@
     scratch += [vmem(BF16, *tensor.shape) for tensor in (conv_first, conv_middle, conv_last)]
     scratch += [vmem(F32, *vector.shape) for vector in affine]
     scratch += [vmem(F32, rows, LANES), vmem(F32, 9, rows, LANES)]
-    scratch += [vmem(BF16, 2, rows, across), vmem(BF16, channels, rows), vmem(F32, rows, across)]
+    if geo.scattered:
+        x_shapes = [(wide // 2, geo.shares[2], rows)] * 2
+    else:
+        x_shapes = [(channels, rows), (CHUNK, LANES)]
+    scratch += [vmem(BF16, 2, rows, across), *[vmem(BF16, *shape) for shape in x_shapes]]
+    scratch += [vmem(F32, rows, across)]
     scratch += [vmem(F32, rows, half), vmem(F32, rows, half), vmem(F32, rows, across)]
     scratch += [vmem(F32, rows, half)] * 2
     scratch += [vmem(BF16, 2, rows, half)] * 2 + [vmem(BF16, hidden, rows)] * 2
@@ -667,17 +760,25 @@
         vmem(F32, wide, 2, half),
         vmem(F32, wide, 2, half),
     ]
-    scratch += [vmem(F32, *shape) for shape in weight_shapes]
-    if geo.scattered:
+    total_shapes = list(weight_shapes)
+    if geo.scattered:
+        total_shapes[2] = (wide // 2, geo.shares[2], half)
+    scratch += [vmem(F32, *shape) for shape in total_shapes]
+    if geo.scattered:
+        scratch += [vmem(BF16, rows, half)] * 5
+        scratch += [vmem(BF16, rows, LANES)] + [vmem(BF16, rows, half)] * 4
+        scratch += [vmem(BF16, hidden, rows), vmem(BF16, *x_shapes[0]), vmem(F32, guarded, half)]
+        scratch += [vmem(BF16, rows, LANES)]
+        scratch += [vmem(BF16, wide // 2, geo.shares[0], across)] * 2
         for share, shape in zip(geo.shares, weight_shapes):
-            for many in (wide // 2, wide // 4, wide // 4 - 1):
+            for many in (wide // 4, wide // 4 - 1):
                 scratch += [vmem(BF16, many, share, shape[1])] * 2
     scratch += [vmem(F32, *shape) for shape in (share_shapes if geo.scattered else [(8, LANES)] * 3)]
     scratch += [vmem(F32, *vector.shape) for vector in affine]
     dma = pltpu.SemaphoreType.DMA
     scratch += [dma((18,)), dma((15,)), dma((8,)), dma((8,)), dma((6,)), dma((6,))]
     if geo.scattered:
-        scratch += [dma((3, 3)), dma((3, 3))]
+        scratch += [dma((3, 3, wide // 4))] * 2 + [dma((8,))] * 2
 
     anywhere = pl.BlockSpec(memory_space=pl.ANY)
     results = pl.pallas_call(
@@ -690,6 +791,14 @@
             collective_id=0, has_side_effects=True, vmem_limit_bytes=60 * 2**20
         ),
     )(*operands)
+    results = pl.pallas_call(
+        functools.partial(copy_kernel, len(results)),
+        out_shape=[jax.ShapeDtypeStruct(result.shape, result.dtype) for result in results],
+        in_specs=[anywhere] * len(results),
+        out_specs=[anywhere] * len(results),
+        scratch_shapes=[vmem(result.dtype, *result.shape) for result in results]
+        + [dma((2, len(results)))],
+    )(*results)
     images = [as_maps(rows, like) for rows, like in zip(results[0:6], maps * 2)]
     last_grad, middle_grad, first_grad = results[6:9]
     if not geo.scattered:

time: 122 us -> 87.7 us (0.72)
  Pallas kernels: 106 us -> 86.7 us
  local copies, waits for them, and re-layouts: 14.1 us -> 0 us
    pallas_call x1, Pallas kernels: 106 us -> 84 us  [run_block(): pl.pallas_call(functools.partial(block_kernel, geo), out_shape=out_shapes...]
    unnamed x37 -> x0, local copies, waits for them, and re-layouts: 14.1 us -> none
    pallas_call x0 -> x1, Pallas kernels: none -> 2.72 us  [run_block(): pl.pallas_call(functools.partial(copy_kernel, len(results)), out_shape=[j...]
where the time goes in v2:
time: 87.7 us; the launch traced here: 87.6 us
  Pallas kernels  86.7 us (99%)
    pallas_call x1, Pallas kernels, run_block(): pl.pallas_call(functools.partial(block_kernel, geo), out_shape=out_shapes...  84 us
    pallas_call x1, Pallas kernels, run_block(): pl.pallas_call(functools.partial(copy_kernel, len(results)), out_shape=[j...  2.72 us

profile of v2, /device:TPU:0, one launch (start us, length us, event | category | flops | bytes accessed | tf_op | source)
XLA Modules:
  0.0 87.6 jit_solution(11821260169167925203)
XLA Ops:
  0.7 84.0 %shard_map.271 = (bf16[25,4,1024]{2,1,0:T(4,128)(2,1)}, bf16[36,4,1024]{2,1,0:T(4,128)(2,1)}, bf16[49,4,1024]{2,1,0:T(4,128)(2,1)}, bf16[25,4,1024]{2,1,0:T(4,12...) custom-call(s32[1,3]{1,0:T(1,128)} %refs_0_.1, ...), custom_call_target="tpu_custom_call" | custom-call | tf_op jit(solution)/shard_map/pallas_call | solution.py:784
  84.7 2.7 %shard_map.272 = (bf16[25,4,1024]{2,1,0:T(4,128)(2,1)}, bf16[36,4,1024]{2,1,0:T(4,128)(2,1)}, bf16[49,4,1024]{2,1,0:T(4,128)(2,1)}, bf16[25,4,1024]{2,1,0:T(4,12...) custom-call(bf16[25,4,1024]{2,1,0:T(4,128)(2,1)} %get-tuple-element., ...), custom_call_target="tpu_custom_call" | custom-call | tf_op jit(solution)/shard_map/pallas_call | solution.py:794

commit v3 on v2

--- a/solution.py
+++ b/solution.py
@@ -55,10 +55,6 @@
     return lax.dot_general(left, right, (((1,), (0,)), ((), ())), preferred_element_type=F32)
 
 
-def dot_turned(left, right):
-    return lax.dot_general(left, right, (((1,), (1,)), ((), ())), preferred_element_type=F32)
-
-
 def gelu_parts(value):
     share = 0.5 + 0.5 * lax.erf(value * 0.7071067811865476)
     slope = share + value * (jnp.exp(value * value * -0.5) * 0.3989422804014327)
@@ -84,6 +80,7 @@
     affine_outs = take(6)
     raw_x, raw_cot, raw_out, raw_grad = take(3), take(3), take(3), take(3)
     conv_first, conv_middle, conv_last = take(3)
+    first_turned, middle_turned, last_turned = take(3)
     affine = take(6)
     live, shift_masks = take(2)
     x_all, x_kept, x_given, cot_rows = take(4)
@@ -248,7 +245,6 @@
         pending[name] = copy.wait_recv
         pending[name, "sent"] = copy.wait_send
 
-    greeted = False
     for group in range(3):
         settle(("x", group))
         rows, real, start = geo.padded[group], geo.real[group], geo.starts[group]
@@ -258,13 +254,12 @@
         mask = spread(live[start : start + rows, :], geo.wide_half)
         place = x_all.at[core, pl.ds(start, rows)]
         place[...] = (value * mask).astype(BF16)
-        if not greeted:
-            pl.semaphore_wait(barrier, wide)
-            greeted = True
-        exchange(("x other", group), group, place, place)
-
     settle("first")
     norm_one[...] = dot(x_all[core], conv_first[span(core * geo.wide_half, geo.wide_half), :])
+    pl.semaphore_wait(barrier, wide)
+    for group in range(3):
+        place = x_all.at[core, pl.ds(geo.starts[group], geo.padded[group])]
+        exchange(("x other", group), group, place, place)
     settle(*(("x other", group) for group in range(3)))
     norm_one[...] += dot(x_all[other], conv_first[span(other * geo.wide_half, geo.wide_half), :])
 
@@ -394,13 +389,17 @@
     half_one, half_two = (norm_one_half, norm_two_half) if geo.scattered else (None, None)
     activate(norm_one, half_one, slope_act_one, hidden_one, centre_one, scale_one, gain_one, shift_one)
     exchange("hidden one", 3, hidden_one.at[core], hidden_one.at[core])
-    settle("middle", "hidden one")
+    settle("middle")
 
     whole = slice(GUARD, GUARD + geo.rows)
     for position in range(9):
-        low = position * geo.hidden
-        parts[position, whole, :] = dot(hidden_one[0], conv_middle[low : low + half, :]) + dot(
-            hidden_one[1], conv_middle[low + half : low + geo.hidden, :]
+        parts[position, whole, :] = dot(
+            hidden_one[core], conv_middle[span(position * geo.hidden + core * half, half), :]
+        )
+    settle("hidden one")
+    for position in range(9):
+        parts[position, whole, :] += dot(
+            hidden_one[other], conv_middle[span(position * geo.hidden + other * half, half), :]
         )
     for group, value in enumerate(fold_parts(lambda position: position)):
         norm_two[geo.starts[group] : geo.starts[group] + geo.padded[group], :] = value
@@ -416,16 +415,23 @@
         if rows > real:
             value = jnp.concatenate([value, jnp.zeros((rows - real, geo.wide_half), F32)], axis=0)
         cot_rows[start : start + rows, :] = value * spread(live[start : start + rows, :], geo.wide_half)
+    for index in range(18):
+        middle_turned[index] = conv_middle[index * half : (index + 1) * half, :].T
     centre_two, scale_two, _ = get_moments(1, half)
     activate(norm_two, half_two, slope_act_two, hidden_two, centre_two, scale_two, gain_two, shift_two)
     exchange("hidden two", 4, hidden_two.at[core], hidden_two.at[core])
-    settle("last", "hidden two")
-    norm_three[...] = dot(hidden_two[0], conv_last[0:half, :]) + dot(hidden_two[1], conv_last[half:, :])
+    settle("last")
+    norm_three[...] = dot(hidden_two[core], conv_last[span(core * half, half), :])
+    settle("hidden two")
+    norm_three[...] += dot(hidden_two[other], conv_last[span(other * half, half), :])
     send_moments(2, norm_three, geo.wide_half)
     if geo.scattered:
         to_pair("turned", 3, turned_one, pair_turned)
     for index in range(2):
         turned_two[index * half : (index + 1) * half, :] = hidden_two[index].T
+    for index in range(2):
+        last_turned[index] = conv_last[index * half : (index + 1) * half, :].T
+        first_turned[index] = conv_first[index * geo.wide_half : (index + 1) * geo.wide_half, :].T
     centre_three, scale_three, inverse_wide = get_moments(2, geo.wide_half)
 
     def finish(rows, carry):
@@ -506,30 +512,29 @@
         pending["scatter", which, stage, piece] = copy.wait_recv
         pending["scatter sent", which, stage, piece] = copy.wait_send
 
-    def rs_first():
-        for piece in (1, 0):
-            low = piece * quarter
-
-            def fill(slot):
-                send_a[slot] = owned(0, slot + wide // 2).astype(BF16)
-
-            over_slots(low, low + quarter, fill)
-            part = pl.ds(low, quarter)
-            rs_start(0, 0, piece, send_a.at[part], recv_a.at[part], wide // 2)
-
-    def rs_second(which):
+    def rs_first(piece):
+        low = piece * quarter
+
+        def fill(slot):
+            send_a[slot] = owned(0, slot + wide // 2).astype(BF16)
+
+        over_slots(low, low + quarter, fill)
+        part = pl.ds(low, quarter)
+        rs_start(0, 0, piece, send_a.at[part], recv_a.at[part], wide // 2)
+
+    high_slots = list(reversed(range(quarter // 2, quarter)))
+    low_slots = list(reversed(range(quarter // 2)))
+    far_slots = [slot for slot in high_slots + low_slots if slot]
+
+    def rs_second(which, slots):
         send_b, recv_b = staged[which][0:2]
-        if which == 0:
-            settle(("scatter", 0, 0, 1))
-        for slot in reversed(range(quarter)):
+        for slot in slots:
             send_b[slot] = reduced(which, slot + quarter).astype(BF16)
             rs_start(which, 1, slot, send_b.at[slot], recv_b.at[slot], quarter)
 
-    def rs_third(which):
+    def rs_third(which, slots):
         _, recv_b, send_c, recv_c = staged[which]
-        if which == 0:
-            settle(("scatter", 0, 0, 0))
-        for slot in reversed(range(1, quarter)):
+        for slot in slots:
             settle(("scatter", which, 1, slot))
             send_c[slot - 1] = (reduced(which, slot) + recv_b[slot].astype(F32)).astype(BF16)
             rs_start(which, 2, slot, send_c.at[slot - 1], recv_c.at[slot - 1], slot)
@@ -548,12 +553,14 @@
     slopes(
         up_three, norm_three, live, slope_three, scale_three, gain_three, sums_three, inverse_wide, geo.wide_half
     )
-    send_two[...] = dot_turned(slope_three[...], conv_last[span(other * half, half), :]).astype(BF16)
+    send_two[...] = dot(slope_three[...], last_turned[other]).astype(BF16)
     exchange("back two", 5, send_two, recv_two)
     totals[0][...] = dot(turned_two[...], slope_three[...])
-    if not geo.scattered:
+    if geo.scattered:
+        rs_first(1)
+    else:
         store(totals[0], weight_outs[0])
-    up_two[...] = dot_turned(slope_three[...], conv_last[span(core * half, half), :])
+    up_two[...] = dot(slope_three[...], last_turned[core])
     give_affine(2, sums_three)
     settle("back two")
 
@@ -572,7 +579,9 @@
     send_sums(4, *back_sums(up_two, half_up_two, recv_two, slope_act_two, norm_two))
     if geo.scattered:
         to_pair("up two", 5, up_two_half, pair_up_two)
-        rs_first()
+        rs_first(0)
+        settle(("scatter", 0, 0, 1))
+        rs_second(0, high_slots + low_slots)
         settle(("pair", "live"), ("pair", "norm two"), ("pair", "turned"))
     sums_two = get_sums(4)
     slopes(up_two, norm_two, live, slope_two, scale_two, gain_two, sums_two, inverse, half, shifted_src)
@@ -591,24 +600,14 @@
                 value = value * spread(shift_masks[flipped, start : start + rows, :], half)
             shifted[start : start + rows, :] = value.astype(BF16)
 
-    def back_parts(low):
+    def back_parts(which_half):
         for position in range(9):
-            rows = pl.ds(pl.multiple_of(position * geo.hidden + low, half), half)
-            parts[position, whole, :] = dot_turned(slope_two[...], conv_middle[rows, :])
+            parts[position, whole, :] = dot(slope_two[...], middle_turned[2 * position + which_half])
         return fold_parts(lambda position: 8 - position)
 
-    for group, value in enumerate(back_parts(other * half)):
+    for group, value in enumerate(back_parts(other)):
         send_one[geo.starts[group] : geo.starts[group] + geo.padded[group], :] = value.astype(BF16)
     exchange("back one", 6, send_one, recv_one)
-    for group, value in enumerate(back_parts(core * half)):
-        up_one[geo.starts[group] : geo.starts[group] + geo.padded[group], :] = value
-    give_affine(1, sums_two)
-    settle("back one")
-
-    send_sums(5, *back_sums(up_one, half_up_one, recv_one, slope_act_one, norm_one))
-    if geo.scattered:
-        to_pair("up one", 6, up_one_half, pair_up_one)
-        rs_second(0)
     for position in range(9):
         place = slice(position * geo.hidden, (position + 1) * geo.hidden)
         shift_into(shifted_src, position)
@@ -618,11 +617,23 @@
             value = value + dot(pair_turned[...], shifted[...])
         totals[1][place, :] = value
     if geo.scattered:
-        rs_second(1)
-        rs_third(0)
-        settle(("pair", "norm one"), ("pair", "x low"), ("pair", "x high"))
+        rs_second(1, high_slots)
+        settle(("scatter", 0, 0, 0))
+        rs_third(0, far_slots[:-1])
     else:
         store(totals[1], weight_outs[1])
+    for group, value in enumerate(back_parts(core)):
+        up_one[geo.starts[group] : geo.starts[group] + geo.padded[group], :] = value
+    give_affine(1, sums_two)
+    settle("back one")
+
+    send_sums(5, *back_sums(up_one, half_up_one, recv_one, slope_act_one, norm_one))
+    if geo.scattered:
+        to_pair("up one", 6, up_one_half, pair_up_one)
+        rs_second(1, low_slots)
+        rs_third(0, far_slots[-1:])
+        rs_third(1, far_slots[:-1])
+        settle(("pair", "norm one"), ("pair", "x low"), ("pair", "x high"))
     sums_one = get_sums(5)
     slopes(up_one, norm_one, live, slope_one, scale_one, gain_one, sums_one, inverse, half)
     if geo.scattered:
@@ -633,17 +644,14 @@
         share = geo.shares[2]
         for slot in reversed(range(wide // 2)):
             totals[2][slot] = dot(x_kept[slot], slope_one[...]) + dot(pair_x[slot], pair_slope[...])
-        rs_second(2)
+        rs_second(2, high_slots + low_slots)
+        rs_third(1, far_slots[-1:])
     else:
         totals[2][...] = dot(x_kept[...], slope_one[...])
         store(totals[2], weight_outs[2])
-    send_in[...] = dot_turned(
-        slope_one[...], conv_first[span(other * geo.wide_half, geo.wide_half), :]
-    ).astype(BF16)
+    send_in[...] = dot(slope_one[...], first_turned[other]).astype(BF16)
     exchange("back in", 7, send_in, recv_in)
-    if geo.scattered:
-        rs_third(1)
-    up_three[...] += dot_turned(slope_one[...], conv_first[span(core * geo.wide_half, geo.wide_half), :])
+    up_three[...] += dot(slope_one[...], first_turned[core])
     give_affine(0, sums_one)
     settle("back in")
     for group in range(3):
@@ -653,7 +661,7 @@
         raw_grad[group][...] = value.astype(BF16)
         store(raw_grad[group], in_grads[group])
     if geo.scattered:
-        rs_third(2)
+        rs_third(2, far_slots)
         rs_last(0)
         rs_last(1)
         rs_last(2)
@@ -737,6 +745,7 @@
     rows, guarded = geo.rows, geo.rows + 2 * GUARD
     scratch = [vmem(BF16, *shape) for shape in raw_shapes * 4]
     scratch += [vmem(BF16, *tensor.shape) for tensor in (conv_first, conv_middle, conv_last)]
+    scratch += [vmem(BF16, 2, half, across), vmem(BF16, 18, half, half), vmem(BF16, 2, across, half)]
     scratch += [vmem(F32, *vector.shape) for vector in affine]
     scratch += [vmem(F32, rows, LANES), vmem(F32, 9, rows, LANES)]
     if geo.scattered:

time: 87.7 us -> 85.8 us (0.978)
  Pallas kernels: 86.7 us -> 84.8 us
    pallas_call x1, Pallas kernels: 84 us -> 82.1 us  [run_block(): pl.pallas_call(functools.partial(block_kernel, geo), out_shape=out_shapes...]
where the time goes in v3:
time: 85.8 us; the launch traced here: 85.6 us
  Pallas kernels  84.8 us (99%)
    pallas_call x1, Pallas kernels, run_block(): pl.pallas_call(functools.partial(block_kernel, geo), out_shape=out_shapes...  82.1 us
    pallas_call x1, Pallas kernels, run_block(): pl.pallas_call(functools.partial(copy_kernel, len(results)), out_shape=[j...  2.72 us

profile of v3, /device:TPU:0, one launch (start us, length us, event | category | flops | bytes accessed | tf_op | source)
XLA Modules:
  0.0 85.6 jit_solution(10980802576624819268)
XLA Ops:
  0.7 82.1 %shard_map.271 = (bf16[25,4,1024]{2,1,0:T(4,128)(2,1)}, bf16[36,4,1024]{2,1,0:T(4,128)(2,1)}, bf16[49,4,1024]{2,1,0:T(4,128)(2,1)}, bf16[25,4,1024]{2,1,0:T(4,12...) custom-call(s32[1,3]{1,0:T(1,128)} %refs_0_.1, ...), custom_call_target="tpu_custom_call" | custom-call | tf_op jit(solution)/shard_map/pallas_call | solution.py:793
  82.7 2.7 %shard_map.272 = (bf16[25,4,1024]{2,1,0:T(4,128)(2,1)}, bf16[36,4,1024]{2,1,0:T(4,128)(2,1)}, bf16[49,4,1024]{2,1,0:T(4,128)(2,1)}, bf16[25,4,1024]{2,1,0:T(4,12...) custom-call(bf16[25,4,1024]{2,1,0:T(4,128)(2,1)} %get-tuple-element., ...), custom_call_target="tpu_custom_call" | custom-call | tf_op jit(solution)/shard_map/pallas_call | solution.py:803

commit v4 on v3

--- a/solution.py
+++ b/solution.py
@@ -190,7 +190,7 @@
     def live_rows(rows, width):
         return spread(live[rows, :], width)
 
-    def over_rows(body, init, unroll=1):
+    def over_rows(body, init, unroll=4):
         return lax.fori_loop(
             0, geo.chunks, lambda step, carry: body(span(step * CHUNK, CHUNK), carry), init, unroll=unroll
         )

time: 85.8 us -> 83.7 us (0.976)
  Pallas kernels: 84.8 us -> 82.7 us
    pallas_call x1, Pallas kernels: 82.1 us -> 80 us  [run_block(): pl.pallas_call(functools.partial(block_kernel, geo), out_shape=out_shapes...]
where the time goes in v4:
time: 83.7 us; the launch traced here: 83.5 us
  Pallas kernels  82.7 us (99%)
    pallas_call x1, Pallas kernels, run_block(): pl.pallas_call(functools.partial(block_kernel, geo), out_shape=out_shapes...  80 us
    pallas_call x1, Pallas kernels, run_block(): pl.pallas_call(functools.partial(copy_kernel, len(results)), out_shape=[j...  2.72 us

profile of v4, /device:TPU:0, one launch (start us, length us, event | category | flops | bytes accessed | tf_op | source)
XLA Modules:
  0.0 83.5 jit_solution(6825204953609065038)
XLA Ops:
  0.7 80.0 %shard_map.271 = (bf16[25,4,1024]{2,1,0:T(4,128)(2,1)}, bf16[36,4,1024]{2,1,0:T(4,128)(2,1)}, bf16[49,4,1024]{2,1,0:T(4,128)(2,1)}, bf16[25,4,1024]{2,1,0:T(4,12...) custom-call(s32[1,3]{1,0:T(1,128)} %refs_0_.1, ...), custom_call_target="tpu_custom_call" | custom-call | tf_op jit(solution)/shard_map/pallas_call | solution.py:793
  80.7 2.7 %shard_map.272 = (bf16[25,4,1024]{2,1,0:T(4,128)(2,1)}, bf16[36,4,1024]{2,1,0:T(4,128)(2,1)}, bf16[49,4,1024]{2,1,0:T(4,128)(2,1)}, bf16[25,4,1024]{2,1,0:T(4,12...) custom-call(bf16[25,4,1024]{2,1,0:T(4,128)(2,1)} %get-tuple-element., ...), custom_call_target="tpu_custom_call" | custom-call | tf_op jit(solution)/shard_map/pallas_call | solution.py:803

commit v5 on v4

--- a/solution.py
+++ b/solution.py
@@ -190,7 +190,7 @@
     def live_rows(rows, width):
         return spread(live[rows, :], width)
 
-    def over_rows(body, init, unroll=4):
+    def over_rows(body, init, unroll=geo.chunks):
         return lax.fori_loop(
             0, geo.chunks, lambda step, carry: body(span(step * CHUNK, CHUNK), carry), init, unroll=unroll
         )

time: 83.7 us -> 83 us (level)
  no operation moved by 1% of the time
where the time goes in v5:
time: 83 us; the launch traced here: 82.9 us
  Pallas kernels  82.1 us (99%)
    pallas_call x1, Pallas kernels, run_block(): pl.pallas_call(functools.partial(block_kernel, geo), out_shape=out_shapes...  79.3 us
    pallas_call x1, Pallas kernels, run_block(): pl.pallas_call(functools.partial(copy_kernel, len(results)), out_shape=[j...  2.72 us

profile of v5, /device:TPU:0, one launch (start us, length us, event | category | flops | bytes accessed | tf_op | source)
XLA Modules:
  0.0 82.9 jit_solution(6628733634669964901)
XLA Ops:
  0.7 79.3 %shard_map.271 = (bf16[25,4,1024]{2,1,0:T(4,128)(2,1)}, bf16[36,4,1024]{2,1,0:T(4,128)(2,1)}, bf16[49,4,1024]{2,1,0:T(4,128)(2,1)}, bf16[25,4,1024]{2,1,0:T(4,12...) custom-call(s32[1,3]{1,0:T(1,128)} %refs_0_.1, ...), custom_call_target="tpu_custom_call" | custom-call | tf_op jit(solution)/shard_map/pallas_call | solution.py:793
  80.0 2.7 %shard_map.272 = (bf16[25,4,1024]{2,1,0:T(4,128)(2,1)}, bf16[36,4,1024]{2,1,0:T(4,128)(2,1)}, bf16[49,4,1024]{2,1,0:T(4,128)(2,1)}, bf16[25,4,1024]{2,1,0:T(4,12...) custom-call(bf16[25,4,1024]{2,1,0:T(4,128)(2,1)} %get-tuple-element., ...), custom_call_target="tpu_custom_call" | custom-call | tf_op jit(solution)/shard_map/pallas_call | solution.py:803
